TPU v7x, 32 devices: a whole 2x2x4 slice. The times are simulated.
32 devices in a mesh: enc: 4 (over y, core), seq: 8 (over z, x).
Axes of the slice: x: 2, y: 2, z: 4, core: 2. Of those that a mesh axis runs over, the one named last changes fastest.
Arguments:
- hidden: bfloat16 [2048, 4096], P('seq'), may hold values from -6 to 6
- dec_gain: float32 [4096], replicated, may hold values from 0.1 to 1.9
- cca_query: bfloat16 [4096, 4096], P(None, 'enc'), may hold values from -0.5 to 0.5
- cca_key: bfloat16 [896, 4096], P(None, 'enc'), may hold values from -0.5 to 0.5
- cca_value: bfloat16 [896, 4096], P(None, 'enc'), may hold values from -0.1875 to 0.1875
- cca_out: bfloat16 [4096, 4096], P('enc'), may hold values from -0.09375 to 0.09375
- neighbours: bfloat16 [8, 8, 128, 896], P('seq', 'enc'), may hold values from -6 to 6
- enc_gain: float32 [896], replicated, may hold values from 0.1 to 1.9
- enc_query: bfloat16 [896, 896], P('enc'), may hold values from -0.5 to 0.5
- enc_key: bfloat16 [896, 896], P('enc'), may hold values from -0.5 to 0.5
- enc_value: bfloat16 [896, 896], P('enc'), may hold values from -0.1875 to 0.1875
- enc_output: bfloat16 [896, 896], P('enc'), may hold values from -0.1875 to 0.1875
- enc_cotangent: bfloat16 [8, 8, 128, 896], P('seq', 'enc'), may hold values from -6 to 6
- neighbour_ids: int32 [32, 2], P('seq'), may hold values from 0 to 7, as said below
Outputs:
- mixed: bfloat16 [2048, 4096], P('seq', 'enc')
- d_neighbours: bfloat16 [8, 8, 128, 896], P('seq', 'enc')
- grad_query: float32 [896, 896], P(('enc', 'seq'))
- grad_key: float32 [896, 896], P(('enc', 'seq'))
- grad_value: float32 [896, 896], P(('enc', 'seq'))
- grad_out: float32 [896, 896], P(('enc', 'seq'))
Inputs may be any that keep to these rules, and one draw needn't show every extreme that they name: `neighbour_ids`: within each aligned block of 4 stretches every position 0 to 7 appears exactly once.
All inputs are finite; a program needn't handle non-finite values.
Results may differ from a plain program's by a relative error of at most 0.025.
Values may be sent and summed in bfloat16 or wider, within the bound.
A program may use at most 192 MiB of HBM per device.

v0:
```python
import jax
import jax.numpy as jnp
from jax import lax
from jax.experimental import pallas as pl
from jax.experimental.pallas import tpu as pltpu
from jax.sharding import PartitionSpec as P

HD = 128
DE = 896
EHEADS = 14
EHD = 64
C = 64
R = 128
K = 2
SEQ_LEN = 2048


EPS = 1e-06


def shifted(value, axis, steps):
    count = lax.axis_size(axis)
    initial, last = (max(0, -steps), min(count, count - steps))
    return lax.ppermute(value, axis, [(source, source + steps) for source in range(initial, last)])


def matmul(former, latter):
    return jnp.dot(former, latter, preferred_element_type=jnp.float32)


def inner_rows(former, latter):
    return lax.dot_general(
        former, latter, (((0,), (0,)), ((), ())), preferred_element_type=jnp.float32
    )


def outer_cols(former, latter):
    return lax.dot_general(
        former, latter, (((1,), (1,)), ((), ())), preferred_element_type=jnp.float32
    )


def two_heads(block):
    low = lax.broadcasted_iota(jnp.int32, block.shape, 1) < EHD
    zero = jnp.zeros_like(block)
    return jnp.concatenate([jnp.where(low, block, zero), jnp.where(low, zero, block)], axis=0)


def join_heads(stacked):
    half = stacked.shape[0] // 2
    low = lax.broadcasted_iota(jnp.int32, (half, stacked.shape[1]), 1) < EHD
    return jnp.where(low, stacked[:half], stacked[half:])


def softmax(scores):
    powers = jnp.exp(scores - jnp.max(scores, axis=-1, keepdims=True))
    return powers / jnp.sum(powers, axis=-1, keepdims=True)


def units(rows):
    pairs = EHEADS * EHD // 128
    return [
        (n * pairs + h, slice(n * R, (n + 1) * R), slice(h * 128, (h + 1) * 128))
        for n in range(rows // R)
        for h in range(pairs)
    ]


def forward_kernel(
    x_ref, gain_ref, qk_ref, vo_ref, enc_ref, normed_ref, q_ref, k_ref, v_ref, p_ref, ctx_ref
):
    x = x_ref[...].astype(jnp.float32)
    inv_rms = lax.rsqrt(jnp.mean(x * x, axis=-1, keepdims=True) + EPS)
    normed_ref[...] = (x * inv_rms * gain_ref[...]).astype(jnp.bfloat16)
    normed = normed_ref[...]
    q_ref[...] = matmul(normed, qk_ref[0]).astype(jnp.bfloat16)
    k_ref[...] = matmul(normed, qk_ref[1]).astype(jnp.bfloat16)
    v_ref[...] = matmul(normed, vo_ref[0]).astype(jnp.bfloat16)
    for at, rows, lanes in units(x_ref.shape[0]):
        scores = outer_cols(two_heads(q_ref[rows, lanes]), k_ref[rows, lanes]) * EHD ** (-0.5)
        weight = softmax(scores)
        p_ref[at] = weight
        ctx_ref[rows, lanes] = join_heads(
            matmul(weight.astype(jnp.bfloat16), v_ref[rows, lanes])
        ).astype(jnp.bfloat16)
    enc_ref[...] = (
        x_ref[...].astype(jnp.float32) + matmul(ctx_ref[...], vo_ref[1])
    ).astype(jnp.bfloat16)


def backward_kernel(
    x_ref,
    gain_ref,
    cot_ref,
    qk_ref,
    vo_ref,
    normed_ref,
    q_ref,
    k_ref,
    v_ref,
    p_ref,
    ctx_ref,
    order_a_ref,
    order_b_ref,
    dx_ref,
    a_keep,
    a_send,
    b_keep,
    b_send,
    dctx,
    dq,
    dk,
    dv,
):
    half = a_keep.shape[1]

    def emit(which, keep, send, former, latter):
        keep[which] = matmul(former[:half], latter).astype(jnp.bfloat16)
        send[which] = matmul(former[half:], latter).astype(jnp.bfloat16)

    dctx[...] = outer_cols(cot_ref[...], vo_ref[1]).astype(jnp.bfloat16)
    for at, rows, lanes in units(x_ref.shape[0]):
        d_context = two_heads(dctx[rows, lanes])
        weight = p_ref[at]
        d_p = outer_cols(d_context, v_ref[rows, lanes])
        dv[rows, lanes] = inner_rows(weight.astype(jnp.bfloat16), d_context).astype(jnp.bfloat16)
        d_s = (
            weight
            * (d_p - jnp.sum(d_p * weight, axis=-1, keepdims=True))
            * EHD ** (-0.5)
        ).astype(jnp.bfloat16)
        dq[rows, lanes] = join_heads(matmul(d_s, k_ref[rows, lanes])).astype(jnp.bfloat16)
        dk[rows, lanes] = inner_rows(d_s, two_heads(q_ref[rows, lanes])).astype(jnp.bfloat16)
    rows_a = outer_cols(order_a_ref[...], normed_ref[...]).astype(jnp.bfloat16)
    emit(0, a_keep, a_send, rows_a, dv[...])
    rows_o = outer_cols(order_a_ref[...], ctx_ref[...]).astype(jnp.bfloat16)
    emit(1, a_keep, a_send, rows_o, cot_ref[...])
    rows_b = outer_cols(order_b_ref[...], normed_ref[...]).astype(jnp.bfloat16)
    emit(0, b_keep, b_send, rows_b, dq[...])
    emit(1, b_keep, b_send, rows_b, dk[...])
    d_normed = (
        outer_cols(dq[...], qk_ref[0])
        + outer_cols(dk[...], qk_ref[1])
        + outer_cols(dv[...], vo_ref[0])
    )
    scaled = d_normed * gain_ref[...]
    x = x_ref[...].astype(jnp.float32)
    inv_rms = lax.rsqrt(jnp.mean(x * x, axis=-1, keepdims=True) + EPS)
    d_rows = inv_rms * scaled - x * inv_rms**3 * jnp.mean(x * scaled, axis=-1, keepdims=True)
    dx_ref[...] = (cot_ref[...].astype(jnp.float32) + d_rows).astype(jnp.bfloat16)


def decode_kernel(place_ref, q_ref, wk_ref, wv_ref, *refs):
    pieces, (ctx_ref, kv) = refs[:-2], refs[-2:]
    weights = jnp.concatenate([wk_ref[...], wv_ref[...]], axis=1)
    rows = pieces[0].shape[0]
    for at, piece in enumerate(pieces):
        kv[at * rows : (at + 1) * rows, :] = matmul(piece[...], weights).astype(jnp.bfloat16)
    for group in range(q_ref.shape[0] // C):
        span = slice(group * C, (group + 1) * C)
        query = q_ref[span, :]
        blocks = [kv[pl.ds(pl.multiple_of(place_ref[group, i] * R, R), R), :] for i in range(K)]
        scores = jnp.concatenate([outer_cols(query, b[:, :HD]) for b in blocks], axis=1)
        weight = softmax(scores * HD ** (-0.5)).astype(jnp.bfloat16)
        total = matmul(weight[:, :R], blocks[0][:, HD:])
        for i in range(1, K):
            total = total + matmul(weight[:, i * R : (i + 1) * R], blocks[i][:, HD:])
        ctx_ref[span, :] = total.astype(jnp.bfloat16)


LIMIT = 52 * 1024 * 1024


def decode(place, queries, key_weight, value_weight, pieces):
    count, width = queries.shape
    whole = [pl.BlockSpec(piece.shape, lambda h: (0, 0)) for piece in pieces]
    rows = sum(piece.shape[0] for piece in pieces)
    column = lambda h: (0, h)
    flops = 2 * rows * DE * 2 * width + 4 * count * K * R * width
    return pl.pallas_call(
        decode_kernel,
        grid=(width // HD,),
        out_shape=jax.ShapeDtypeStruct((count, width), jnp.bfloat16),
        in_specs=[
            pl.BlockSpec(memory_space=pltpu.SMEM),
            pl.BlockSpec((count, HD), column),
            pl.BlockSpec((DE, HD), column),
            pl.BlockSpec((DE, HD), column),
        ]
        + whole,
        out_specs=pl.BlockSpec((count, HD), column),
        scratch_shapes=[pltpu.VMEM((rows, 2 * HD), jnp.bfloat16)],
        compiler_params=pltpu.CompilerParams(vmem_limit_bytes=LIMIT),
        cost_estimate=pl.CostEstimate(
            flops=2 * flops, bytes_accessed=rows * DE * 2 + 4 * DE * width, transcendentals=0
        ),
    )(place, queries, key_weight, value_weight, *pieces)


def one_call(kernel, outs, scratch, args, flops):
    vmem = pl.BlockSpec(memory_space=pltpu.VMEM)
    size = sum(a.size * a.dtype.itemsize for a in (*args, *outs))
    return pl.pallas_call(
        kernel,
        out_shape=outs,
        in_specs=[vmem] * len(args),
        out_specs=[vmem] * len(outs),
        scratch_shapes=scratch,
        compiler_params=pltpu.CompilerParams(vmem_limit_bytes=LIMIT),
        cost_estimate=pl.CostEstimate(flops=flops, bytes_accessed=size, transcendentals=0),
    )(*args)


def swap(value, axis, distance):
    count = lax.axis_size(axis)
    return lax.ppermute(value, axis, [(i, i ^ distance) for i in range(count)])


def ordered(flag, mine, other, axis):
    low = jnp.where(flag == 0, mine, other)
    high = jnp.where(flag == 0, other, mine)
    return jnp.concatenate([low, high], axis=axis)


def gather_rows(blocks, core, chip, pair):
    half = blocks.shape[1] // 2
    sibling = swap(blocks, "enc", 1)
    part = lax.dynamic_slice_in_dim(blocks, pair * half, half, 1)
    across = swap(part, "enc", 2)
    beside = swap(across, "seq", 1)
    far = ordered(pair, across, beside, 1)
    far_sibling = swap(far, "enc", 1)
    near = ordered(core, blocks, sibling, 1)
    away = ordered(core, far, far_sibling, 1)
    return ordered(chip, near, away, 1)


def pick(value, index, axis):
    return lax.dynamic_index_in_dim(value, index, axis, keepdims=False)


def on_device(
    hidden,
    dec_gain,
    cca_query,
    cca_key,
    cca_value,
    cca_out,
    neighbours,
    enc_gain,
    enc_query,
    enc_key,
    enc_value,
    enc_output,
    enc_cotangent,
    neighbour_ids,
):
    enc_count, seq_count = lax.axis_size("enc"), lax.axis_size("seq")
    enc_at, seq_at = lax.axis_index("enc"), lax.axis_index("seq")
    core, chip, pair, line = enc_at % 2, enc_at // 2, seq_at % 2, seq_at // 2
    lines = seq_count // 2
    first = gather_rows(jnp.stack([enc_query, enc_key]), core, chip, pair)
    second = gather_rows(jnp.stack([enc_value, enc_output]), core, chip, pair)
    local_count = neighbours.shape[1]
    rows = local_count * R
    x_rows = neighbours.reshape(rows, DE)
    cotangent = enc_cotangent.reshape(rows, DE)
    gain = enc_gain.reshape(1, DE)
    low = jax.ShapeDtypeStruct((rows, DE), jnp.bfloat16)
    soft = jax.ShapeDtypeStruct((rows // R * (DE // 128), 2 * R, R), jnp.float32)
    encoded, normed_rows, enc_q, enc_k, enc_v, enc_p, enc_ctx = one_call(
        forward_kernel,
        [low, low, low, low, low, soft, low],
        [],
        (x_rows, gain, first, second),
        12 * rows * DE * DE,
    )
    own_rows = DE // (enc_count * seq_count)
    target = jnp.arange(DE, dtype=jnp.int32)
    inner, block = target % own_rows, target // own_rows
    ahead = (line + block % lines) % lines
    low_bit, mid_bit, top_bit = (
        block // lines % 2,
        block // lines // 2 % 2,
        block // lines // 4,
    )

    def order(chip_bit, pair_bit):
        device = ((chip ^ chip_bit) * 2 + (core ^ top_bit)) * seq_count + ahead * 2 + (
            pair ^ pair_bit
        )
        return (target[None, :] == (device * own_rows + inner)[:, None]).astype(jnp.bfloat16)

    part = jax.ShapeDtypeStruct((2, DE // 2, DE), jnp.bfloat16)
    space = [pltpu.VMEM((rows, DE), jnp.bfloat16)] * 4
    d_input, a_keep, a_send, b_keep, b_send = one_call(
        backward_kernel,
        [low, part, part, part, part],
        space,
        (
            x_rows,
            gain,
            cotangent,
            first,
            second,
            normed_rows,
            enc_q,
            enc_k,
            enc_v,
            enc_p,
            enc_ctx,
            order(mid_bit, low_bit),
            order(low_bit, mid_bit),
        ),
        28 * rows * DE * DE,
    )

    def added(former, latter):
        return (former.astype(jnp.float32) + latter.astype(jnp.float32)).astype(jnp.bfloat16)

    def reduce_pair(keep, send, routes):
        came = swap(send, "enc", 1)
        for axis, distance in routes:
            half = keep.shape[1] // 2
            send = added(keep[:, half:], came[:, half:])
            keep = added(keep[:, :half], came[:, :half])
            came = swap(send, axis, distance)
        return added(keep, came)

    held = jnp.concatenate(
        [
            reduce_pair(a_keep, a_send, (("enc", 2), ("seq", 1))),
            reduce_pair(b_keep, b_send, (("seq", 1), ("enc", 2))),
        ],
        axis=0,
    ).reshape(4, lines, own_rows, DE)
    total = held[:, 0].astype(jnp.float32)
    for step in range(1, lines):
        moved = [(i, (i + 2 * step) % seq_count) for i in range(seq_count)]
        total = total + lax.ppermute(held[:, step], "seq", moved).astype(jnp.float32)
    total = total / (local_count * enc_count * seq_count)
    grads = (total[2], total[3], total[0], total[1])

    head_width = cca_key.shape[1]
    sibling = swap(encoded, "enc", 1)
    across = swap(encoded, "enc", 2)
    across_sibling = swap(across, "enc", 1)
    pieces = (encoded, sibling, across, across_sibling)
    owner = neighbour_ids // local_count
    place = (owner ^ enc_at) * local_count + neighbour_ids % local_count
    stretch_count = neighbour_ids.shape[0]
    tokens = [piece.reshape(local_count, R, DE) for piece in pieces]

    def chosen(at):
        value = tokens[0][0]
        for i in range(1, enc_count * local_count):
            value = jnp.where(at == i, tokens[i // local_count][i % local_count], value)
        return value

    last = jnp.concatenate([chosen(place[stretch_count - 1, i]) for i in range(K)], axis=0)
    earlier_rows = shifted(last, "seq", 1)
    hidden_f = hidden.astype(jnp.float32)
    inv_rms = lax.rsqrt(jnp.mean(hidden_f * hidden_f, axis=-1, keepdims=True) + EPS)
    normed = (hidden_f * inv_rms * dec_gain).astype(jnp.bfloat16)
    token_count, model_width = hidden.shape
    padded = jnp.concatenate(
        [
            jnp.zeros((1, model_width), jnp.bfloat16),
            normed,
            jnp.zeros((C - 1, model_width), jnp.bfloat16),
        ],
        axis=0,
    )
    queries = matmul(padded, cca_query).astype(jnp.bfloat16)
    own_context = decode(place, queries[C:], cca_key, cca_value, pieces)
    in_order = jnp.arange(K, dtype=jnp.int32).reshape(1, K)
    early_context = decode(in_order, queries[:C], cca_key, cca_value, (earlier_rows,))
    context = jnp.concatenate([early_context, own_context], axis=0)[1 : token_count + 1]
    position = (
        seq_at * token_count + jnp.arange(token_count, dtype=jnp.int32) + C
    ) % SEQ_LEN
    context = jnp.where((position >= C - 1)[:, None], context, jnp.zeros_like(context))
    wide = cca_out.shape[1] // 2
    slice_width = wide // 2

    def out_half(which):
        columns = lax.dynamic_slice_in_dim(cca_out, which * wide, wide, 1)
        return matmul(context, columns).astype(jnp.bfloat16).reshape(token_count, 2, slice_width)

    far_part = out_half(1 - chip)
    far_sum = added(
        pick(far_part, core, 1), swap(pick(far_part, 1 - core, 1), "enc", 1)
    )
    landed = swap(far_sum, "enc", 2)
    near_part = out_half(chip)
    near_sent = swap(pick(near_part, 1 - core, 1), "enc", 1)
    branch = (
        pick(near_part, core, 1).astype(jnp.float32)
        + near_sent.astype(jnp.float32)
        + landed.astype(jnp.float32)
    )
    residual = lax.dynamic_slice_in_dim(hidden, enc_at * slice_width, slice_width, 1)
    mixed = (residual.astype(jnp.float32) + branch).astype(jnp.bfloat16)
    return (mixed, d_input.reshape(neighbours.shape), grads[0], grads[1], grads[2], grads[3])


def solution(mesh):
    return jax.shard_map(
        on_device,
        mesh=mesh,
        in_specs=(
            P("seq", None),
            P(),
            P(None, "enc"),
            P(None, "enc"),
            P(None, "enc"),
            P("enc", None),
            P("seq", "enc", None, None),
            P(),
            P("enc", None),
            P("enc", None),
            P("enc", None),
            P("enc", None),
            P("seq", "enc", None, None),
            P("seq", None),
        ),
        out_specs=(
            P("seq", "enc"),
            P("seq", "enc", None, None),
            P(("enc", "seq"), None),
            P(("enc", "seq"), None),
            P(("enc", "seq"), None),
            P(("enc", "seq"), None),
        ),
        check_vma=False,
    )
```

profile of v0, /device:TPU:0, one launch (start us, length us, event | category | flops | bytes accessed | tf_op | source)
XLA Modules:
  0.0 187.1 jit_solution(17912332849579486821)
XLA Ops:
  0.7 1.9 %fusion.29 = bf16[2,112,896]{2,1,0:T(8,128)(2,1)} fusion(s32[]{:T(128)S(6)} %select_n.367, bf16[1,224,896]{2,1,0:T(8,128)(2,1)} %bitcast.66, bf16[1,224,896]{2,1,0:T(8,128)(2,1)} %bitcast.69), kind=kLoop, calls=%fused_computation.72 | loop fusion | flops 802816 | bytes 1204228 | tf_op jit(solution)/shard_map/stack | solution.py:263
  2.6 3.0 %collective-permute-start.5 = (bf16[2,112,896]{2,1,0:T(8,128)(2,1)}, bf16[2,112,896]{2,1,0:T(8,128)(2,1)}, u32[]{:S(2)}, u32[]{:S(2)}) collective-permute-start(bf16[2,112,896]{2,1,0:T(8,128)(2,1)} %fusion.29), channel_id=1, source_target_pairs={{0,16},{8,24},{16,0},{24,8},{1,17},{9,25},{17,1},{25,9},{2,18},{10... | collective-permute-start | bytes 1204232 | tf_op jit(solution)/shard_map/ppermute | solution.py:216
  5.5 2.1 %pad_maximum_fusion.7 = bf16[2,224,896]{2,1,0:T(8,128)(2,1)} fusion(bf16[1,224,896]{2,1,0:T(8,128)(2,1)} %bitcast.70, bf16[1,224,896]{2,1,0:T(8,128)(2,1)} %bitcast.67), kind=kLoop, calls=%fused_computation.46 | loop fusion | flops 401408 | bytes 1605632 | tf_op jit(solution)/shard_map/stack | solution.py:263
  7.6 0.8 fusion.30
  8.6 1.0 pad_maximum_fusion.6
  9.9 0.5 fusion
  10.5 0.7 fusion.2
  11.3 7.2 %fusion.19 = bf16[320,1024]{1,0:T(8,128)(2,1)} fusion(bf16[4096,1024]{1,0:T(8,128)(2,1)} %param.16, bf16[256,4096]{1,0:T(8,128)(2,1)S(1)} %fusion.2, bf16[320]{0:T(512)(128)(2,1)S(1)} %pad.28.clone, bf16[320]{0:T(512)(128)(2,1)S(1)} %pad.26.clone), kind=kOutput, calls=%fused_computation.33 | convolution fusion | flops 2692546560 | bytes 11142400 | tf_op jit(solution)/shard_map/dot_general | solution.py:28
  18.6 1.8 collective-permute-start.6
  20.5 0.6 fusion.66
  21.1 2.5 %collective-permute-done.1 = bf16[2,112,896]{2,1,0:T(8,128)(2,1)S(1)} collective-permute-done((bf16[2,112,896]{2,1,0:T(8,128)(2,1)}, bf16[2,112,896]{2,1,0:T(8,128)(2,1)S(1)}, u32[]{:S(2)}, u32[]{:S(2)}) %collective-permute-start.1) | collective-permute-done | bytes 401440 | tf_op jit(solution)/shard_map/ppermute | solution.py:216
  23.6 1.7 collective-permute-start.2
  34.4 0.9 slice.164.q_ref
  35.3 1.9 slice.171.q_ref
  37.2 1.2 broadcast_select_fusion.13
  38.6 0.5 collective-permute-done.2
  39.1 1.1 broadcast_select_fusion.15
  40.4 1.3 broadcast_select_fusion.7
  41.7 1.3 broadcast_select_fusion.11
  43.4 0.6 broadcast_select_fusion.1
  44.3 0.6 broadcast_select_fusion.3
  44.9 3.0 %pad_maximum_fusion = (bf16[2,896,896]{2,1,0:T(8,128)(2,1)}, bf16[2,896,896]{2,1,0:T(8,128)(2,1)}) fusion(bf16[2,448,896]{2,1,0:T(8,128)(2,1)S(1)} %get-tuple-element.37, bf16[2,448,896]{2,1,0:T(8,128)(2,1)S(1)} %get-tuple-element.36, bf16[2,448,896]{2,1,0:T(8,128)(2,1)S(1)} %get-tuple-element.35, bf16[2,448,896]{2,1,0:T(8,128)(2,1)S(1)} %get-tuple-element.34), kind=kLoop, calls=%fused_computation.9 | loop fusion | flops 12845056 | bytes 12845056 | tf_op jit(solution)/shard_map/concatenate | solution.py:222
  47.9 7.5 %shard_map.181 = (bf16[256,896]{1,0:T(8,128)(2,1)S(1)}, bf16[256,896]{1,0:T(8,128)(2,1)S(1)}, bf16[256,896]{1,0:T(8,128)(2,1)S(1)}, bf16[256,896]{1,0:T(8,128)(2...) custom-call(bf16[256,896]{1,0:T(8,128)(2,1)} %bitcast.63, ...), custom_call_target="tpu_custom_call" | custom-call | flops 2466250752 | bytes 11472384 | tf_op jit(solution)/shard_map/pallas_call | solution.py:203
  55.3 0.8 copy-done.2
  56.1 1.6 collective-permute-start.8
  57.8 1.5 fusion.7.order_a_ref
  59.3 1.5 fusion.8.order_b_ref
  61.0 8.0 %collective-permute-done.8.refs_2_ = bf16[256,896]{1,0:T(8,128)(2,1)S(1)} collective-permute-done((bf16[256,896]{1,0:T(8,128)(2,1)S(1)}, bf16[256,896]{1,0:T(8,128)(2,1)S(1)}, u32[]{:S(2)}, u32[]{:S(2)}) %collective-permute-start.8) | collective-permute-done | bytes 458784 | tf_op jit(solution)/shard_map/ppermute | solution.py:216
  69.0 17.2 %shard_map.184 = (bf16[256,896]{1,0:T(8,128)(2,1)}, bf16[2,448,896]{2,1,0:T(8,128)(2,1)}, bf16[2,448,896]{2,1,0:T(8,128)(2,1)}, bf16[2,448,896]{2,1,0:T(8,128)(2,1)}, bf16[2,448,896]{2,1,0:T(8,128)(2,1)}) custom-call(bf16[256,896]{1,0:T(8,128)(2,1)S(1)} %bitcast.64, f32[1,896]{1,0:T(1,128)S(1)} %reshape.239.gain_ref, bf16[256,896]{1,0:T(8,128)(2,1)S(1)} %bitcast.65, ...), custom_call_target="tpu_custom_call" | custom-call | flops 5754585088 | bytes 21564928 | tf_op jit(solution)/shard_map/pallas_call | solution.py:203
  86.2 0.5 collective-permute-start.15
  87.0 3.7 %collective-permute-start.11 = (bf16[256,896]{1,0:T(8,128)(2,1)S(1)}, bf16[256,896]{1,0:T(8,128)(2,1)S(1)}, u32[]{:S(2)}, u32[]{:S(2)}) collective-permute-start(bf16[256,896]{1,0:T(8,128)(2,1)S(1)} %pad_maximum_fusion.12), channel_id=1, source_target_pairs={{0,1},{1,2},{2,3},{3,4},{4,5},{5,6},{6,7},{8,9},{9,10},{10,11},{11... | collective-permute-start | bytes 1376264 | tf_op jit(solution)/shard_map/ppermute | solution.py:24
  90.7 19.7 %shard_map.183 = bf16[256,1024]{1,0:T(8,128)(2,1)} custom-call(s32[4,2]{1,0:T(4,128)S(1)} %fusion.57.place_ref, bf16[256,1024]{1,0:T(8,128)(2,1)} %slice.171.q_ref, bf16[896,1024]{1,0:T(8,128)(2,1)} %wk_ref.3, bf16[896,1024]{1,0:T(8,128)(2,1)} %wv_ref.3, bf16[256,896]{1,0:T(8,128)(2,1)S(1)} %get-tuple-element.18.refs_0_, ...), custom_call_target="tpu_custom_call" | custom-call | flops 8053063680 | bytes 5505024 | tf_op jit(solution)/shard_map/pallas_call | solution.py:180
  110.4 8.7 %shard_map.182 = bf16[64,1024]{1,0:T(8,128)(2,1)S(1)} custom-call(s32[1,2]{1,0:T(1,128)S(1)} %iota.34.place_ref, bf16[64,1024]{1,0:T(8,128)(2,1)S(1)} %slice.164.q_ref, bf16[896,1024]{1,0:T(8,128)(2,1)} %wk_ref.3, bf16[896,1024]{1,0:T(8,128)(2,1)} %wv_ref.3, bf16[256,896]{1,0:T(8,128)(2,1)S(1)} %collective-permute-done.11.refs_0_), custom_call_target="tpu_custom_call" | custom-call | flops 2013265920 | bytes 4128768 | tf_op jit(solution)/shard_map/pallas_call | solution.py:180
  119.1 4.5 %fusion.13 = bf16[256,2048]{1,0:T(8,128)(2,1)} fusion(bf16[1024,4096]{1,0:T(8,128)(2,1)} %param.19, s32[]{:T(128)S(6)} %select_n.410, bf16[256,1024]{1,0:T(8,128)(2,1)S(1)} %copy-done.14, bf16[64,1024]{1,0:T(8,128)(2,1)S(1)} %shard_map.182, pred[256]{0:T(512)(128)(4,1)S(1)} %fusion.61), kind=kOutput, calls=%fused_computation.19 | convolution fusion | flops 1075576832 | bytes 5898500 | tf_op jit(solution)/shard_map/dot_general | solution.py:28
  123.6 1.8 reshape.240
  125.4 3.5 %add_convert_fusion.3 = (bf16[2,224,896]{2,1,0:T(8,128)(2,1)}, bf16[2,224,896]{2,1,0:T(8,128)(2,1)}) fusion(bf16[2,448,896]{2,1,0:T(8,128)(2,1)} %collective-permute-done.15, bf16[2,448,896]{2,1,0:T(8,128)(2,1)} %get-tuple-element.26), kind=kLoop, calls=%fused_computation.28 | loop fusion | flops 3211264 | bytes 4816896 | tf_op jit(solution)/shard_map/convert_element_type | solution.py:319
  129.0 1.4 collective-permute-start.16
  130.4 3.1 %add_convert_fusion.1 = (bf16[2,224,896]{2,1,0:T(8,128)(2,1)}, bf16[2,224,896]{2,1,0:T(8,128)(2,1)}) fusion(bf16[2,448,896]{2,1,0:T(8,128)(2,1)} %collective-permute-done.18, bf16[2,448,896]{2,1,0:T(8,128)(2,1)S(1)} %copy-done.10), kind=kLoop, calls=%fused_computation.26 | loop fusion | flops 3211264 | bytes 4816896 | tf_op jit(solution)/shard_map/convert_element_type | solution.py:319
  133.5 1.5 collective-permute-start.19
  135.0 4.5 %fusion.16 = bf16[256,2048]{1,0:T(8,128)(2,1)} fusion(bf16[1024,4096]{1,0:T(8,128)(2,1)} %param.19, s32[]{:T(128)S(6)} %select_n.413, bf16[256,1024]{1,0:T(8,128)(2,1)S(1)} %copy-done.15, bf16[64,1024]{1,0:T(8,128)(2,1)S(1)} %shard_map.182, pred[256]{0:T(512)(128)(4,1)S(1)} %fusion.61), kind=kOutput, calls=%fused_computation.20 | convolution fusion | flops 1075576832 | bytes 5898500 | tf_op jit(solution)/shard_map/dot_general | solution.py:28
  139.6 2.6 %reshape.241 = bf16[256,2,1024]{2,1,0:T(2,128)(2,1)} reshape(bf16[256,2048]{1,0:T(8,128)(2,1)} %fusion.16) | data formatting | bytes 2097152 | tf_op jit(solution)/shard_map/reshape | solution.py:388
  142.2 3.7 %constant_dynamic-slice_fusion.1 = (bf16[256,1,1024]{2,1,0:T(2,128)(2,1)S(1)}, bf16[256,1,1024]{2,1,0:T(2,128)(2,1)S(1)}) fusion(bf16[256,2,1024]{2,1,0:T(2,128)(2,1)} %reshape.241, s32[]{:T(128)S(6)} %select_n.411, s32[]{:T(128)S(6)} %select_n.412), kind=kLoop, calls=%fused_computation.140 | loop fusion | bytes 2097160 | tf_op jit(solution)/shard_map/jit(dynamic_index_in_dim)/dynamic_slice | solution.py:239
  146.2 2.2 %constant_dynamic-slice_fusion.3 = (bf16[256,1,1024]{2,1,0:T(2,128)(2,1)S(1)}, bf16[256,1,1024]{2,1,0:T(2,128)(2,1)S(1)}) fusion(bf16[256,2,1024]{2,1,0:T(2,128)(2,1)S(1)} %reshape.240, s32[]{:T(128)S(6)} %select_n.411, s32[]{:T(128)S(6)} %select_n.412), kind=kLoop, calls=%fused_computation.143 | loop fusion | bytes 2097160 | tf_op jit(solution)/shard_map/jit(dynamic_index_in_dim)/dynamic_slice | solution.py:239
  148.5 0.6 collective-permute-start.12
  149.3 1.1 add_convert_fusion.8
  150.4 1.6 collective-permute-start.17
  151.9 2.0 %collective-permute-done.19 = bf16[2,224,896]{2,1,0:T(8,128)(2,1)} collective-permute-done((bf16[2,224,896]{2,1,0:T(8,128)(2,1)}, bf16[2,224,896]{2,1,0:T(8,128)(2,1)}, u32[]{:S(2)}, u32[]{:S(2)}) %collective-permute-start.19) | collective-permute-done | bytes 802848 | tf_op jit(solution)/shard_map/ppermute | solution.py:216
  154.0 1.1 add_convert_fusion.5
  155.1 0.5 collective-permute-start.20
  155.9 1.7 collective-permute-start.14
  157.6 4.4 %collective-permute-done.17 = bf16[2,112,896]{2,1,0:T(8,128)(2,1)S(1)} collective-permute-done((bf16[2,112,896]{2,1,0:T(8,128)(2,1)S(1)}, bf16[2,112,896]{2,1,0:T(8,128)(2,1)S(1)}, u32[]{:S(2)}, u32[]{:S(2)}) %collective-permute-start.17) | collective-permute-done | bytes 401440 | tf_op jit(solution)/shard_map/ppermute | solution.py:216
  162.0 1.2 add_convert_fusion.7
  163.2 4.2 %collective-permute-done.20 = bf16[2,112,896]{2,1,0:T(8,128)(2,1)S(1)} collective-permute-done((bf16[2,112,896]{2,1,0:T(8,128)(2,1)S(1)}, bf16[2,112,896]{2,1,0:T(8,128)(2,1)S(1)}, u32[]{:S(2)}, u32[]{:S(2)}) %collective-permute-start.20) | collective-permute-done | bytes 401440 | tf_op jit(solution)/shard_map/ppermute | solution.py:216
  167.4 1.2 add_convert_fusion.4
  169.2 1.6 collective-permute-start.21
  170.8 3.2 %collective-permute-start.22 = (bf16[4,28,896]{2,0,1:T(4,128)(2,1)S(1)}, bf16[4,28,896]{2,0,1:T(4,128)(2,1)S(1)}, u32[]{:S(2)}, u32[]{:S(2)}) collective-permute-start(bf16[4,28,896]{2,0,1:T(4,128)(2,1)S(1)} %get-tuple-element.52), channel_id=1, source_target_pairs={{0,4},{1,5},{2,6},{3,7},{4,0},{5,1},{6,2},{7,3},{8,12},{9,13},{10,... | collective-permute-start | bytes 602120 | tf_op jit(solution)/shard_map/ppermute | solution.py:340
  174.0 0.8 collective-permute-start.23
  174.7 1.4 collective-permute-done.14
  176.1 1.3 fusion.27
  177.7 6.2 %collective-permute-done.22 = bf16[4,28,896]{2,0,1:T(4,128)(2,1)S(1)} collective-permute-done((bf16[4,28,896]{2,0,1:T(4,128)(2,1)S(1)}, bf16[4,28,896]{2,0,1:T(4,128)(2,1)S(1)}, u32[]{:S(2)}, u32[]{:S(2)}) %collective-permute-start.22) | collective-permute-done | bytes 200736 | tf_op jit(solution)/shard_map/ppermute | solution.py:340
  184.4 0.7 copy.61
  185.1 0.7 copy.62
  185.7 0.7 copy.63
  186.4 0.7 copy.64
  (81 shorter events, 4.6 us)
Async XLA Ops:
  0.6 7.0 %copy-start.6 = (bf16[224,896]{1,0:T(8,128)(2,1)S(1)}, bf16[224,896]{1,0:T(8,128)(2,1)}, u32[]{:S(2)}) copy-start(bf16[224,896]{1,0:T(8,128)(2,1)} %param.22) | copy-start | bytes 1204228
  0.6 7.0 %copy-start.7 = (bf16[224,896]{1,0:T(8,128)(2,1)S(1)}, bf16[224,896]{1,0:T(8,128)(2,1)}, u32[]{:S(2)}) copy-start(bf16[224,896]{1,0:T(8,128)(2,1)} %param.23) | copy-start | bytes 1204228
  2.5 7.4 %copy-start.3 = (bf16[256,4096]{1,0:T(8,128)(2,1)S(1)}, bf16[256,4096]{1,0:T(8,128)(2,1)}, u32[]{:S(2)}) copy-start(bf16[256,4096]{1,0:T(8,128)(2,1)} %param.14) | copy-start | bytes 6291460
  2.6 16.1 %collective-permute-start.5 = (bf16[2,112,896]{2,1,0:T(8,128)(2,1)}, bf16[2,112,896]{2,1,0:T(8,128)(2,1)}, u32[]{:S(2)}, u32[]{:S(2)}) collective-permute-start(bf16[2,112,896]{2,1,0:T(8,128)(2,1)} %fusion.29), channel_id=1, source_target_pairs={{0,16},{8,24},{16,0},{24,8},{1,17},{9,25},{17,1},{25,9},{2,18},{10... | collective-permute-start | bytes 1204232 | tf_op jit(solution)/shard_map/ppermute | solution.py:216
  7.6 32.8 %collective-permute-start.4 = (bf16[2,224,896]{2,1,0:T(8,128)(2,1)}, bf16[2,224,896]{2,1,0:T(8,128)(2,1)}, u32[]{:S(2)}, u32[]{:S(2)}) collective-permute-start(bf16[2,224,896]{2,1,0:T(8,128)(2,1)} %pad_maximum_fusion.7), channel_id=1, source_target_pairs={{0,8},{8,0},{16,24},{24,16},{1,9},{9,1},{17,25},{25,17},{2,10},{10... | collective-permute-start | bytes 2408456 | tf_op jit(solution)/shard_map/ppermute | solution.py:216
  8.4 2.1 %copy-start.11 = (f32[4096]{0:T(1024)S(1)}, f32[4096]{0:T(1024)}, u32[]{:S(2)}) copy-start(f32[4096]{0:T(1024)} %param.15) | copy-start | bytes 49156
  8.4 15.2 %collective-permute-start.1 = (bf16[2,112,896]{2,1,0:T(8,128)(2,1)}, bf16[2,112,896]{2,1,0:T(8,128)(2,1)S(1)}, u32[]{:S(2)}, u32[]{:S(2)}) collective-permute-start(bf16[2,112,896]{2,1,0:T(8,128)(2,1)} %fusion.30), channel_id=1, source_target_pairs={{0,16},{8,24},{16,0},{24,8},{1,17},{9,25},{17,1},{25,9},{2,18},{10... | collective-permute-start | bytes 1204232 | tf_op jit(solution)/shard_map/ppermute | solution.py:216
  9.6 32.2 %collective-permute-start = (bf16[2,224,896]{2,1,0:T(8,128)(2,1)}, bf16[2,224,896]{2,1,0:T(8,128)(2,1)}, u32[]{:S(2)}, u32[]{:S(2)}) collective-permute-start(bf16[2,224,896]{2,1,0:T(8,128)(2,1)} %pad_maximum_fusion.6), channel_id=1, source_target_pairs={{0,8},{8,0},{16,24},{24,16},{1,9},{9,1},{17,25},{25,17},{2,10},{10... | collective-permute-start | bytes 2408456 | tf_op jit(solution)/shard_map/ppermute | solution.py:216
  11.3 7.3 %copy-start.13 = (s32[4,2]{0,1:T(2,128)S(1)}, s32[4,2]{0,1:T(2,128)}, u32[]{:S(2)}) copy-start(s32[4,2]{0,1:T(2,128)} %param.27) | copy-start | bytes 100
  11.3 25.9 %copy-start.12 = (f32[896]{0:T(1024)S(1)}, f32[896]{0:T(1024)}, u32[]{:S(2)}) copy-start(f32[896]{0:T(1024)} %param.21) | copy-start | bytes 10756
  18.6 18.6 %collective-permute-start.6 = (bf16[2,112,896]{2,1,0:T(8,128)(2,1)}, bf16[2,112,896]{2,1,0:T(8,128)(2,1)}, u32[]{:S(2)}, u32[]{:S(2)}) collective-permute-start(bf16[2,112,896]{2,1,0:T(8,128)(2,1)} %collective-permute-done.5), channel_id=1, source_target_pairs={{0,1},{1,0},{2,3},{3,2},{4,5},{5,4},{6,7},{7,6},{8,9},{9,8},{10,11... | collective-permute-start | bytes 1204232 | tf_op jit(solution)/shard_map/ppermute | solution.py:216
  23.6 15.5 %collective-permute-start.2 = (bf16[2,112,896]{2,1,0:T(8,128)(2,1)S(1)}, bf16[2,112,896]{2,1,0:T(8,128)(2,1)}, u32[]{:S(2)}, u32[]{:S(2)}) collective-permute-start(bf16[2,112,896]{2,1,0:T(8,128)(2,1)S(1)} %collective-permute-done.1), channel_id=1, source_target_pairs={{0,1},{1,0},{2,3},{3,2},{4,5},{5,4},{6,7},{7,6},{8,9},{9,8},{10,11... | collective-permute-start | bytes 1204232 | tf_op jit(solution)/shard_map/ppermute | solution.py:216
  38.4 2.0 %copy-start.4 = (bf16[224,896]{1,0:T(8,128)(2,1)S(1)}, bf16[224,896]{1,0:T(8,128)(2,1)}, u32[]{:S(2)}) copy-start(bf16[224,896]{1,0:T(8,128)(2,1)} %param.24) | copy-start | bytes 1204228
  38.4 2.0 %copy-start.5 = (bf16[224,896]{1,0:T(8,128)(2,1)S(1)}, bf16[224,896]{1,0:T(8,128)(2,1)}, u32[]{:S(2)}) copy-start(bf16[224,896]{1,0:T(8,128)(2,1)} %param.25) | copy-start | bytes 1204228
  38.5 4.6 %collective-permute-start.7 = (bf16[2,224,896]{2,1,0:T(8,128)(2,1)S(1)}, bf16[2,224,896]{2,1,0:T(8,128)(2,1)S(1)}, u32[]{:S(2)}, u32[]{:S(2)}) collective-permute-start(bf16[2,224,896]{2,1,0:T(8,128)(2,1)S(1)} %pad_maximum_fusion.9), channel_id=1, source_target_pairs={{0,8},{8,0},{16,24},{24,16},{1,9},{9,1},{17,25},{25,17},{2,10},{10... | collective-permute-start | bytes 2408456 | tf_op jit(solution)/shard_map/ppermute | solution.py:216
  40.3 3.7 %collective-permute-start.3 = (bf16[2,224,896]{2,1,0:T(8,128)(2,1)S(1)}, bf16[2,224,896]{2,1,0:T(8,128)(2,1)S(1)}, u32[]{:S(2)}, u32[]{:S(2)}) collective-permute-start(bf16[2,224,896]{2,1,0:T(8,128)(2,1)S(1)} %pad_maximum_fusion.8), channel_id=1, source_target_pairs={{0,8},{8,0},{16,24},{24,16},{1,9},{9,1},{17,25},{25,17},{2,10},{10... | collective-permute-start | bytes 2408456 | tf_op jit(solution)/shard_map/ppermute | solution.py:216
  55.3 0.8 copy-start.2
  56.1 12.9 %copy-start = (bf16[1,2,128,896]{3,2,1,0:T(8,128)(2,1)S(1)}, bf16[1,2,128,896]{3,2,1,0:T(8,128)(2,1)}, u32[]{:S(2)}) copy-start(bf16[1,2,128,896]{3,2,1,0:T(8,128)(2,1)} %param.20) | copy-start | bytes 1376260
  56.1 12.9 %copy-start.1 = (bf16[1,2,128,896]{3,2,1,0:T(8,128)(2,1)S(1)}, bf16[1,2,128,896]{3,2,1,0:T(8,128)(2,1)}, u32[]{:S(2)}) copy-start(bf16[1,2,128,896]{3,2,1,0:T(8,128)(2,1)} %param.26) | copy-start | bytes 1376260
  56.1 12.9 %collective-permute-start.8 = (bf16[256,896]{1,0:T(8,128)(2,1)S(1)}, bf16[256,896]{1,0:T(8,128)(2,1)S(1)}, u32[]{:S(2)}, u32[]{:S(2)}) collective-permute-start(bf16[256,896]{1,0:T(8,128)(2,1)S(1)} %get-tuple-element.18.refs_0_), channel_id=1, source_target_pairs={{0,16},{8,24},{16,0},{24,8},{1,17},{9,25},{17,1},{25,9},{2,18},{10... | collective-permute-start | bytes 1376264 | tf_op jit(solution)/shard_map/ppermute | solution.py:216
  60.8 26.0 %collective-permute-start.10 = (bf16[256,896]{1,0:T(8,128)(2,1)S(1)}, bf16[256,896]{1,0:T(8,128)(2,1)S(1)}, u32[]{:S(2)}, u32[]{:S(2)}) collective-permute-start(bf16[256,896]{1,0:T(8,128)(2,1)S(1)} %get-tuple-element.18.refs_0_), channel_id=1, source_target_pairs={{0,8},{8,0},{16,24},{24,16},{1,9},{9,1},{17,25},{25,17},{2,10},{10... | collective-permute-start | bytes 1376264 | tf_op jit(solution)/shard_map/ppermute | solution.py:216
  69.0 17.8 %collective-permute-start.9 = (bf16[256,896]{1,0:T(8,128)(2,1)S(1)}, bf16[256,896]{1,0:T(8,128)(2,1)S(1)}, u32[]{:S(2)}, u32[]{:S(2)}) collective-permute-start(bf16[256,896]{1,0:T(8,128)(2,1)S(1)} %collective-permute-done.8.refs_2_), channel_id=1, source_target_pairs={{0,8},{8,0},{16,24},{24,16},{1,9},{9,1},{17,25},{25,17},{2,10},{10... | collective-permute-start | bytes 1376264 | tf_op jit(solution)/shard_map/ppermute | solution.py:216
  86.2 39.2 %collective-permute-start.15 = (bf16[2,448,896]{2,1,0:T(8,128)(2,1)}, bf16[2,448,896]{2,1,0:T(8,128)(2,1)}, u32[]{:S(2)}, u32[]{:S(2)}) collective-permute-start(bf16[2,448,896]{2,1,0:T(8,128)(2,1)} %get-tuple-element.27), channel_id=1, source_target_pairs={{0,8},{8,0},{16,24},{24,16},{1,9},{9,1},{17,25},{25,17},{2,10},{10... | collective-permute-start | bytes 4816904 | tf_op jit(solution)/shard_map/ppermute | solution.py:216
  86.7 43.6 %collective-permute-start.18 = (bf16[2,448,896]{2,1,0:T(8,128)(2,1)}, bf16[2,448,896]{2,1,0:T(8,128)(2,1)}, u32[]{:S(2)}, u32[]{:S(2)}) collective-permute-start(bf16[2,448,896]{2,1,0:T(8,128)(2,1)} %get-tuple-element.29), channel_id=1, source_target_pairs={{0,8},{8,0},{16,24},{24,16},{1,9},{9,1},{17,25},{25,17},{2,10},{10... | collective-permute-start | bytes 4816904 | tf_op jit(solution)/shard_map/ppermute | solution.py:216
  87.0 23.3 %collective-permute-start.11 = (bf16[256,896]{1,0:T(8,128)(2,1)S(1)}, bf16[256,896]{1,0:T(8,128)(2,1)S(1)}, u32[]{:S(2)}, u32[]{:S(2)}) collective-permute-start(bf16[256,896]{1,0:T(8,128)(2,1)S(1)} %pad_maximum_fusion.12), channel_id=1, source_target_pairs={{0,1},{1,2},{2,3},{3,4},{4,5},{5,6},{6,7},{8,9},{9,10},{10,11},{11... | collective-permute-start | bytes 1376264 | tf_op jit(solution)/shard_map/ppermute | solution.py:24
  110.4 8.7 %copy-start.14 = (bf16[256,1024]{1,0:T(8,128)(2,1)S(1)}, bf16[256,1024]{1,0:T(8,128)(2,1)}, u32[]{:S(2)}) copy-start(bf16[256,1024]{1,0:T(8,128)(2,1)} %shard_map.183) | copy-start | bytes 1572868
  125.4 5.0 %copy-start.10 = (bf16[2,448,896]{2,1,0:T(8,128)(2,1)S(1)}, bf16[2,448,896]{2,1,0:T(8,128)(2,1)}, u32[]{:S(2)}) copy-start(bf16[2,448,896]{2,1,0:T(8,128)(2,1)} %get-tuple-element.28) | copy-start | bytes 4816900
  129.0 20.3 %collective-permute-start.16 = (bf16[2,224,896]{2,1,0:T(8,128)(2,1)}, bf16[2,224,896]{2,1,0:T(8,128)(2,1)}, u32[]{:S(2)}, u32[]{:S(2)}) collective-permute-start(bf16[2,224,896]{2,1,0:T(8,128)(2,1)} %get-tuple-element.31), channel_id=1, source_target_pairs={{0,16},{8,24},{16,0},{24,8},{1,17},{9,25},{17,1},{25,9},{2,18},{10... | collective-permute-start | bytes 2408456 | tf_op jit(solution)/shard_map/ppermute | solution.py:216
  130.4 4.7 %copy-start.15 = (bf16[256,1024]{1,0:T(8,128)(2,1)S(1)}, bf16[256,1024]{1,0:T(8,128)(2,1)}, u32[]{:S(2)}) copy-start(bf16[256,1024]{1,0:T(8,128)(2,1)} %shard_map.183) | copy-start | bytes 1572868
  133.5 20.5 %collective-permute-start.19 = (bf16[2,224,896]{2,1,0:T(8,128)(2,1)}, bf16[2,224,896]{2,1,0:T(8,128)(2,1)}, u32[]{:S(2)}, u32[]{:S(2)}) collective-permute-start(bf16[2,224,896]{2,1,0:T(8,128)(2,1)} %get-tuple-element.33), channel_id=1, source_target_pairs={{0,1},{1,0},{2,3},{3,2},{4,5},{5,4},{6,7},{7,6},{8,9},{9,8},{10,11... | collective-permute-start | bytes 2408456 | tf_op jit(solution)/shard_map/ppermute | solution.py:216
  146.1 3.2 %copy-start.8 = (bf16[2,224,896]{2,1,0:T(8,128)(2,1)S(1)}, bf16[2,224,896]{2,1,0:T(8,128)(2,1)}, u32[]{:S(2)}) copy-start(bf16[2,224,896]{2,1,0:T(8,128)(2,1)} %get-tuple-element.30) | copy-start | bytes 2408452
  146.1 9.5 %collective-permute-start.13 = (bf16[256,1024]{1,0:T(8,128)(2,1)S(1)}, bf16[256,1024]{1,0:T(8,128)(2,1)S(1)}, u32[]{:S(2)}, u32[]{:S(2)}) collective-permute-start(bf16[256,1024]{1,0:T(8,128)(2,1)S(1)} %bitcast.81), channel_id=1, source_target_pairs={{0,8},{8,0},{16,24},{24,16},{1,9},{9,1},{17,25},{25,17},{2,10},{10... | collective-permute-start | bytes 1572872 | tf_op jit(solution)/shard_map/ppermute | solution.py:216
  148.3 5.7 %copy-start.9 = (bf16[2,224,896]{2,1,0:T(8,128)(2,1)S(1)}, bf16[2,224,896]{2,1,0:T(8,128)(2,1)}, u32[]{:S(2)}) copy-start(bf16[2,224,896]{2,1,0:T(8,128)(2,1)} %get-tuple-element.32) | copy-start | bytes 2408452
  148.5 26.2 %collective-permute-start.12 = (bf16[256,1024]{1,0:T(8,128)(2,1)S(1)}, bf16[256,1024]{1,0:T(8,128)(2,1)S(1)}, u32[]{:S(2)}, u32[]{:S(2)}) collective-permute-start(bf16[256,1024]{1,0:T(8,128)(2,1)S(1)} %bitcast.80), channel_id=1, source_target_pairs={{0,8},{8,0},{16,24},{24,16},{1,9},{9,1},{17,25},{25,17},{2,10},{10... | collective-permute-start | bytes 1572872 | tf_op jit(solution)/shard_map/ppermute | solution.py:216
  150.4 11.6 %collective-permute-start.17 = (bf16[2,112,896]{2,1,0:T(8,128)(2,1)S(1)}, bf16[2,112,896]{2,1,0:T(8,128)(2,1)S(1)}, u32[]{:S(2)}, u32[]{:S(2)}) collective-permute-start(bf16[2,112,896]{2,1,0:T(8,128)(2,1)S(1)} %add_convert_fusion.8), channel_id=1, source_target_pairs={{0,1},{1,0},{2,3},{3,2},{4,5},{5,4},{6,7},{7,6},{8,9},{9,8},{10,11... | collective-permute-start | bytes 1204232 | tf_op jit(solution)/shard_map/ppermute | solution.py:216
  155.1 12.3 %collective-permute-start.20 = (bf16[2,112,896]{2,1,0:T(8,128)(2,1)S(1)}, bf16[2,112,896]{2,1,0:T(8,128)(2,1)S(1)}, u32[]{:S(2)}, u32[]{:S(2)}) collective-permute-start(bf16[2,112,896]{2,1,0:T(8,128)(2,1)S(1)} %add_convert_fusion.5), channel_id=1, source_target_pairs={{0,16},{8,24},{16,0},{24,8},{1,17},{9,25},{17,1},{25,9},{2,18},{10... | collective-permute-start | bytes 1204232 | tf_op jit(solution)/shard_map/ppermute | solution.py:216
  155.9 20.2 %collective-permute-start.14 = (bf16[256,1024]{1,0:T(8,128)(2,1)S(1)}, bf16[256,1024]{1,0:T(8,128)(2,1)S(1)}, u32[]{:S(2)}, u32[]{:S(2)}) collective-permute-start(bf16[256,1024]{1,0:T(8,128)(2,1)S(1)} %fusion.24), channel_id=1, source_target_pairs={{0,16},{8,24},{16,0},{24,8},{1,17},{9,25},{17,1},{25,9},{2,18},{10... | collective-permute-start | bytes 1572872 | tf_op jit(solution)/shard_map/ppermute | solution.py:216
  169.2 8.5 %collective-permute-start.21 = (bf16[4,28,896]{2,0,1:T(4,128)(2,1)S(1)}, bf16[4,28,896]{2,0,1:T(4,128)(2,1)S(1)}, u32[]{:S(2)}, u32[]{:S(2)}) collective-permute-start(bf16[4,28,896]{2,0,1:T(4,128)(2,1)S(1)} %get-tuple-element.50), channel_id=1, source_target_pairs={{0,2},{1,3},{2,4},{3,5},{4,6},{5,7},{6,0},{7,1},{8,10},{9,11},{10,... | collective-permute-start | bytes 602120 | tf_op jit(solution)/shard_map/ppermute | solution.py:340
  170.8 13.1 %collective-permute-start.22 = (bf16[4,28,896]{2,0,1:T(4,128)(2,1)S(1)}, bf16[4,28,896]{2,0,1:T(4,128)(2,1)S(1)}, u32[]{:S(2)}, u32[]{:S(2)}) collective-permute-start(bf16[4,28,896]{2,0,1:T(4,128)(2,1)S(1)} %get-tuple-element.52), channel_id=1, source_target_pairs={{0,4},{1,5},{2,6},{3,7},{4,0},{5,1},{6,2},{7,3},{8,12},{9,13},{10,... | collective-permute-start | bytes 602120 | tf_op jit(solution)/shard_map/ppermute | solution.py:340
  174.0 10.0 %collective-permute-start.23 = (bf16[4,28,896]{2,0,1:T(4,128)(2,1)S(1)}, bf16[4,28,896]{2,0,1:T(4,128)(2,1)S(1)}, u32[]{:S(2)}, u32[]{:S(2)}) collective-permute-start(bf16[4,28,896]{2,0,1:T(4,128)(2,1)S(1)} %get-tuple-element.51), channel_id=1, source_target_pairs={{0,6},{1,7},{2,0},{3,1},{4,2},{5,3},{6,4},{7,5},{8,14},{9,15},{10,... | collective-permute-start | bytes 602120 | tf_op jit(solution)/shard_map/ppermute | solution.py:340
where the time goes:
time: 188 us; the launch traced here: 187 us
  Pallas kernels  53 us (28%)
  other arithmetic  33.3 us (18%)
  waiting for transfers between devices  29.8 us (16%)
  starting transfers between devices  26 us (14%)
  local copies, waits for them, and re-layouts  18.5 us (10%)
  matrix products  16.3 us (9%)
  between operations  10.2 us (5%)
    pallas_call x2, Pallas kernels, decode(): pl.pallas_call(decode_kernel, grid=(width // HD,), out_shape=jax.ShapeDty...  28.3 us
    pallas_call x2, Pallas kernels, one_call(): pl.pallas_call(kernel, out_shape=outs, in_specs=[vmem] * len(args), out_s...  24.7 us
    ppermute x20, waiting for transfers between devices, swap(): return lax.ppermute(value, axis, [(i, i ^ distance) for i in range(count)])  23.3 us
    ppermute x20, starting transfers between devices, swap(): return lax.ppermute(value, axis, [(i, i ^ distance) for i in range(count)])  16.8 us
    dot_general x3, matrix products, matmul(): return jnp.dot(former, latter, preferred_element_type=jnp.float32)  16.3 us
    convert_element_type x7, other arithmetic, added(): (former.astype(jnp.float32) + latter.astype(jnp.float32)).astype(jnp.bflo...  11.6 us
    select_n x8, other arithmetic, ordered(): low = jnp.where(flag == 0, mine, other)  6.74 us
    ppermute x3, waiting for transfers between devices, on_device(): lax.ppermute(held[:, step], 'seq', moved).astype(jnp.float32)  6.48 us
  transfers between devices with their start and end apart: 24, of which 10 were waited for; matrix products, arithmetic and copies ran while one was open for 31% of the time, Pallas kernels for 24%

commit v1 on v0

--- a/solution.py
+++ b/solution.py
@@ -150,22 +150,36 @@
     dx_ref[...] = (cot_ref[...].astype(jnp.float32) + d_rows).astype(jnp.bfloat16)
 
 
+HEADS_STEP = 2
+
+
 def decode_kernel(place_ref, q_ref, wk_ref, wv_ref, *refs):
     pieces, (ctx_ref, kv) = refs[:-2], refs[-2:]
     weights = jnp.concatenate([wk_ref[...], wv_ref[...]], axis=1)
     rows = pieces[0].shape[0]
     for at, piece in enumerate(pieces):
         kv[at * rows : (at + 1) * rows, :] = matmul(piece[...], weights).astype(jnp.bfloat16)
-    for group in range(q_ref.shape[0] // C):
-        span = slice(group * C, (group + 1) * C)
-        query = q_ref[span, :]
-        blocks = [kv[pl.ds(pl.multiple_of(place_ref[group, i] * R, R), R), :] for i in range(K)]
-        scores = jnp.concatenate([outer_cols(query, b[:, :HD]) for b in blocks], axis=1)
-        weight = softmax(scores * HD ** (-0.5)).astype(jnp.bfloat16)
-        total = matmul(weight[:, :R], blocks[0][:, HD:])
-        for i in range(1, K):
-            total = total + matmul(weight[:, i * R : (i + 1) * R], blocks[i][:, HD:])
-        ctx_ref[span, :] = total.astype(jnp.bfloat16)
+    groups = q_ref.shape[0] // C
+    for head in range(HEADS_STEP):
+        lanes = slice(head * HD, (head + 1) * HD)
+        value_lanes = slice((HEADS_STEP + head) * HD, (HEADS_STEP + head + 1) * HD)
+        scores, spots = [], []
+        for group in range(groups):
+            query = q_ref[group * C : (group + 1) * C, lanes]
+            spot = [pl.ds(pl.multiple_of(place_ref[group, i] * R, R), R) for i in range(K)]
+            scores.append(
+                jnp.concatenate([outer_cols(query, kv[rows, lanes]) for rows in spot], axis=1)
+            )
+            spots.append(spot)
+        weight = softmax(jnp.concatenate(scores, axis=0) * HD ** (-0.5)).astype(jnp.bfloat16)
+        for group in range(groups):
+            part = weight[group * C : (group + 1) * C]
+            total = matmul(part[:, :R], kv[spots[group][0], value_lanes])
+            for i in range(1, K):
+                total = total + matmul(
+                    part[:, i * R : (i + 1) * R], kv[spots[group][i], value_lanes]
+                )
+            ctx_ref[group * C : (group + 1) * C, lanes] = total.astype(jnp.bfloat16)
 
 
 LIMIT = 52 * 1024 * 1024
@@ -179,17 +193,17 @@
     flops = 2 * rows * DE * 2 * width + 4 * count * K * R * width
     return pl.pallas_call(
         decode_kernel,
-        grid=(width // HD,),
+        grid=(width // (HEADS_STEP * HD),),
         out_shape=jax.ShapeDtypeStruct((count, width), jnp.bfloat16),
         in_specs=[
             pl.BlockSpec(memory_space=pltpu.SMEM),
-            pl.BlockSpec((count, HD), column),
-            pl.BlockSpec((DE, HD), column),
-            pl.BlockSpec((DE, HD), column),
+            pl.BlockSpec((count, HEADS_STEP * HD), column),
+            pl.BlockSpec((DE, HEADS_STEP * HD), column),
+            pl.BlockSpec((DE, HEADS_STEP * HD), column),
         ]
         + whole,
-        out_specs=pl.BlockSpec((count, HD), column),
-        scratch_shapes=[pltpu.VMEM((rows, 2 * HD), jnp.bfloat16)],
+        out_specs=pl.BlockSpec((count, HEADS_STEP * HD), column),
+        scratch_shapes=[pltpu.VMEM((rows, 2 * HEADS_STEP * HD), jnp.bfloat16)],
         compiler_params=pltpu.CompilerParams(vmem_limit_bytes=LIMIT),
         cost_estimate=pl.CostEstimate(
             flops=2 * flops, bytes_accessed=rows * DE * 2 + 4 * DE * width, transcendentals=0
@@ -216,27 +230,114 @@
     return lax.ppermute(value, axis, [(i, i ^ distance) for i in range(count)])
 
 
-def ordered(flag, mine, other, axis):
-    low = jnp.where(flag == 0, mine, other)
-    high = jnp.where(flag == 0, other, mine)
-    return jnp.concatenate([low, high], axis=axis)
-
-
-def gather_rows(blocks, core, chip, pair):
-    half = blocks.shape[1] // 2
-    sibling = swap(blocks, "enc", 1)
-    part = lax.dynamic_slice_in_dim(blocks, pair * half, half, 1)
-    across = swap(part, "enc", 2)
-    beside = swap(across, "seq", 1)
-    far = ordered(pair, across, beside, 1)
-    far_sibling = swap(far, "enc", 1)
-    near = ordered(core, blocks, sibling, 1)
-    away = ordered(core, far, far_sibling, 1)
-    return ordered(chip, near, away, 1)
-
-
-def pick(value, index, axis):
-    return lax.dynamic_index_in_dim(value, index, axis, keepdims=False)
+def gather_kernel(q_ref, k_ref, v_ref, o_ref, qk_ref, vo_ref, local_sem, send_sem, recv_sem):
+    enc_at, seq_at = lax.axis_index("enc"), lax.axis_index("seq")
+    pair = seq_at % 2
+    sibling = (enc_at + 1 - 2 * (enc_at % 2), seq_at)
+    across = ((enc_at + 2) % 4, seq_at)
+    beside = (enc_at, seq_at + 1 - 2 * pair)
+    height = q_ref.shape[0]
+    half = height // 2
+    barrier = pltpu.get_barrier_semaphore()
+    for other in (sibling, across, beside):
+        pl.semaphore_signal(barrier, inc=1, device_id=other, device_id_type=pl.DeviceIdType.MESH)
+    pl.semaphore_wait(barrier, 3)
+
+    def place(which, start, count):
+        out = (qk_ref, vo_ref)[which // 2]
+        return out.at[which % 2, pl.ds(pl.multiple_of(start, 16), count)]
+
+    def send(kind, which, source, target, other):
+        copy = pltpu.make_async_remote_copy(
+            src_ref=source,
+            dst_ref=target,
+            send_sem=send_sem.at[kind, which],
+            recv_sem=recv_sem.at[kind, which],
+            device_id=other,
+            device_id_type=pl.DeviceIdType.MESH,
+        )
+        copy.start()
+        return copy
+
+    blocks = (q_ref, k_ref, v_ref, o_ref)
+    far = ((enc_at + 2) % 4) * height
+    mine = enc_at * height
+    copies, crossing, beside_copies = [], [], []
+    for which, block in enumerate(blocks):
+        rows = pl.ds(pl.multiple_of(pair * half, 16), half)
+        crossing.append(
+            send(0, which, block.at[rows], place(which, mine + pair * half, half), across)
+        )
+    for which, block in enumerate(blocks):
+        copies.append(send(1, which, block, place(which, mine, height), sibling))
+    locals_ = []
+    for which, block in enumerate(blocks):
+        copy = pltpu.make_async_copy(block, place(which, mine, height), local_sem.at[which])
+        copy.start()
+        locals_.append(copy)
+    for which in range(4):
+        crossing[which].wait_recv()
+        landed = place(which, far + pair * half, half)
+        beside_copies.append(send(2, which, landed, landed, beside))
+        copies.append(send(3, which, landed, landed, sibling))
+    for which in range(4):
+        beside_copies[which].wait_recv()
+        landed = place(which, far + (1 - pair) * half, half)
+        copies.append(send(4, which, landed, landed, sibling))
+    for copy in crossing + beside_copies:
+        copy.wait_send()
+    for copy in copies:
+        copy.wait()
+    for copy in locals_:
+        copy.wait()
+
+
+def gather_weights(blocks, count):
+    height, width = blocks[0].shape
+    out = jax.ShapeDtypeStruct((2, count * height, width), blocks[0].dtype)
+    anywhere = pl.BlockSpec(memory_space=pl.ANY)
+    return pl.pallas_call(
+        gather_kernel,
+        out_shape=[out, out],
+        in_specs=[anywhere] * 4,
+        out_specs=[anywhere] * 2,
+        scratch_shapes=[
+            pltpu.SemaphoreType.DMA((4,)),
+            pltpu.SemaphoreType.DMA((5, 4)),
+            pltpu.SemaphoreType.DMA((5, 4)),
+        ],
+        compiler_params=pltpu.CompilerParams(
+            collective_id=0, has_side_effects=True, vmem_limit_bytes=LIMIT
+        ),
+    )(*blocks)
+
+
+def project_kernel(_, context_ref, weight_ref, out_ref):
+    out_ref[...] = matmul(context_ref[...], weight_ref[...]).astype(jnp.bfloat16)
+
+
+def project(context, weight, which, count):
+    tokens, depth = context.shape
+    width = weight.shape[1] // count
+    steps = 4
+    tile = width // steps
+    return pl.pallas_call(
+        project_kernel,
+        out_shape=jax.ShapeDtypeStruct((tokens, width), jnp.bfloat16),
+        grid_spec=pltpu.PrefetchScalarGridSpec(
+            num_scalar_prefetch=1,
+            grid=(steps,),
+            in_specs=[
+                pl.BlockSpec((tokens, depth), lambda i, at: (0, 0)),
+                pl.BlockSpec((depth, tile), lambda i, at: (0, at[0] * steps + i)),
+            ],
+            out_specs=pl.BlockSpec((tokens, tile), lambda i, at: (0, i)),
+        ),
+        compiler_params=pltpu.CompilerParams(vmem_limit_bytes=LIMIT),
+        cost_estimate=pl.CostEstimate(
+            flops=2 * tokens * depth * width, bytes_accessed=2 * depth * width, transcendentals=0
+        ),
+    )(which.astype(jnp.int32).reshape(1), context, weight)
 
 
 def on_device(
@@ -259,8 +360,7 @@
     enc_at, seq_at = lax.axis_index("enc"), lax.axis_index("seq")
     core, chip, pair, line = enc_at % 2, enc_at // 2, seq_at % 2, seq_at // 2
     lines = seq_count // 2
-    first = gather_rows(jnp.stack([enc_query, enc_key]), core, chip, pair)
-    second = gather_rows(jnp.stack([enc_value, enc_output]), core, chip, pair)
+    first, second = gather_weights((enc_query, enc_key, enc_value, enc_output), enc_count)
     local_count = neighbours.shape[1]
     rows = local_count * R
     x_rows = neighbours.reshape(rows, DE)
@@ -318,33 +418,18 @@
     def added(former, latter):
         return (former.astype(jnp.float32) + latter.astype(jnp.float32)).astype(jnp.bfloat16)
 
-    def reduce_pair(keep, send, routes):
-        came = swap(send, "enc", 1)
-        for axis, distance in routes:
-            half = keep.shape[1] // 2
-            send = added(keep[:, half:], came[:, half:])
-            keep = added(keep[:, :half], came[:, :half])
-            came = swap(send, axis, distance)
-        return added(keep, came)
-
-    held = jnp.concatenate(
-        [
-            reduce_pair(a_keep, a_send, (("enc", 2), ("seq", 1))),
-            reduce_pair(b_keep, b_send, (("seq", 1), ("enc", 2))),
-        ],
-        axis=0,
-    ).reshape(4, lines, own_rows, DE)
-    total = held[:, 0].astype(jnp.float32)
-    for step in range(1, lines):
-        moved = [(i, (i + 2 * step) % seq_count) for i in range(seq_count)]
-        total = total + lax.ppermute(held[:, step], "seq", moved).astype(jnp.float32)
-    total = total / (local_count * enc_count * seq_count)
-    grads = (total[2], total[3], total[0], total[1])
-
-    head_width = cca_key.shape[1]
+    def cut(keep, came):
+        half = keep.shape[1] // 2
+        return added(keep[:, :half], came[:, :half]), added(keep[:, half:], came[:, half:])
+
+    came_a, came_b = swap(a_send, "enc", 1), swap(b_send, "enc", 1)
+    hidden, a_keep, b_keep = lax.optimization_barrier((hidden, a_keep, b_keep))
+    a_keep, a_send = cut(a_keep, came_a)
+    b_keep, b_send = cut(b_keep, came_b)
+
     sibling = swap(encoded, "enc", 1)
     across = swap(encoded, "enc", 2)
-    across_sibling = swap(across, "enc", 1)
+    across_sibling = swap(encoded, "enc", 3)
     pieces = (encoded, sibling, across, across_sibling)
     owner = neighbour_ids // local_count
     place = (owner ^ enc_at) * local_count + neighbour_ids % local_count
@@ -372,36 +457,48 @@
         axis=0,
     )
     queries = matmul(padded, cca_query).astype(jnp.bfloat16)
-    own_context = decode(place, queries[C:], cca_key, cca_value, pieces)
-    in_order = jnp.arange(K, dtype=jnp.int32).reshape(1, K)
-    early_context = decode(in_order, queries[:C], cca_key, cca_value, (earlier_rows,))
-    context = jnp.concatenate([early_context, own_context], axis=0)[1 : token_count + 1]
+    queries, a_send, b_send = lax.optimization_barrier((queries, a_send, b_send))
+    came_a, came_b = swap(a_send, "enc", 2), swap(b_send, "seq", 1)
+    pool_count = enc_count * local_count
+    in_order = pool_count + jnp.arange(K, dtype=jnp.int32).reshape(1, K)
+    spots = jnp.concatenate([in_order, place.astype(jnp.int32)], axis=0)
+    context = decode(spots, queries, cca_key, cca_value, (*pieces, earlier_rows))
+    context, a_keep, b_keep = lax.optimization_barrier((context, a_keep, b_keep))
+    a_keep, a_send = cut(a_keep, came_a)
+    b_keep, b_send = cut(b_keep, came_b)
+    context = context[1 : token_count + 1]
     position = (
         seq_at * token_count + jnp.arange(token_count, dtype=jnp.int32) + C
     ) % SEQ_LEN
     context = jnp.where((position >= C - 1)[:, None], context, jnp.zeros_like(context))
-    wide = cca_out.shape[1] // 2
-    slice_width = wide // 2
-
-    def out_half(which):
-        columns = lax.dynamic_slice_in_dim(cca_out, which * wide, wide, 1)
-        return matmul(context, columns).astype(jnp.bfloat16).reshape(token_count, 2, slice_width)
-
-    far_part = out_half(1 - chip)
-    far_sum = added(
-        pick(far_part, core, 1), swap(pick(far_part, 1 - core, 1), "enc", 1)
-    )
+    context, a_send, b_send = lax.optimization_barrier((context, a_send, b_send))
+    came_a, came_b = swap(a_send, "seq", 1), swap(b_send, "enc", 2)
+    slice_width = cca_out.shape[1] // enc_count
+
+    def column(source, distance):
+        return project(source, cca_out, enc_at ^ distance, enc_count)
+
+    far_sent = swap(column(context, 3), "enc", 1)
+    far_sum = added(column(context, 2), far_sent)
+    context, far_sum = lax.optimization_barrier((context, far_sum))
     landed = swap(far_sum, "enc", 2)
-    near_part = out_half(chip)
-    near_sent = swap(pick(near_part, 1 - core, 1), "enc", 1)
+    near_sent = swap(column(context, 1), "enc", 1)
+    near = column(context, 0)
+    near, a_keep, b_keep = lax.optimization_barrier((near, a_keep, b_keep))
+    held = jnp.concatenate([added(a_keep, came_a), added(b_keep, came_b)], axis=0).reshape(
+        4, lines, own_rows, DE
+    )
+    total = held[:, 0].astype(jnp.float32)
+    for step in range(1, lines):
+        moved = [(i, (i + 2 * step) % seq_count) for i in range(seq_count)]
+        total = total + lax.ppermute(held[:, step], "seq", moved).astype(jnp.float32)
+    total = total / (local_count * enc_count * seq_count)
     branch = (
-        pick(near_part, core, 1).astype(jnp.float32)
-        + near_sent.astype(jnp.float32)
-        + landed.astype(jnp.float32)
+        near.astype(jnp.float32) + near_sent.astype(jnp.float32) + landed.astype(jnp.float32)
     )
     residual = lax.dynamic_slice_in_dim(hidden, enc_at * slice_width, slice_width, 1)
     mixed = (residual.astype(jnp.float32) + branch).astype(jnp.bfloat16)
-    return (mixed, d_input.reshape(neighbours.shape), grads[0], grads[1], grads[2], grads[3])
+    return (mixed, d_input.reshape(neighbours.shape), total[2], total[3], total[0], total[1])
 
 
 def solution(mesh):

time: 188 us -> 166 us (0.88)
  Pallas kernels: 53 us -> 80.3 us
  other arithmetic: 33.3 us -> 14.2 us
  matrix products: 16.3 us -> 7.23 us
  waiting for transfers between devices: 29.8 us -> 21.2 us
  local copies, waits for them, and re-layouts: 18.5 us -> 12 us
  starting transfers between devices: 26 us -> 20.3 us
    pallas_call x2 -> x6, Pallas kernels: 28.3 us -> 55.4 us  [the longest x1 29.8 us: gather_weights(): pl.pallas_call(gather_kernel, out_shape=[out, out], in_specs=[anywhere] *...]
    ppermute x20 -> x12, waiting for transfers between devices: 23.3 us -> 4.03 us  [swap(): return lax.ppermute(value, axis, [(i, i ^ distance) for i in range(count)])]
    dot_general x3 -> x1, matrix products: 16.3 us -> 7.23 us  [matmul(): return jnp.dot(former, latter, preferred_element_type=jnp.float32)]
    convert_element_type x7, other arithmetic: 11.6 us -> 4.73 us  [added(): (former.astype(jnp.float32) + latter.astype(jnp.float32)).astype(jnp.bflo...]
    ppermute x20 -> x12, starting transfers between devices: 16.8 us -> 10.2 us  [swap(): return lax.ppermute(value, axis, [(i, i ^ distance) for i in range(count)])]
    dynamic_slice x2 -> x0, local copies, waits for them, and re-layouts: 5.88 us -> none  [pick(): return lax.dynamic_index_in_dim(value, index, axis, keepdims=False)]
    another operation x4 -> x0, other arithmetic: 5.76 us -> none  [the longest x2 3.97 us: on_device(): second = gather_rows(jnp.stack([enc_value, enc_output]), core, chip, pair)]
    select_n x8 -> x1, other arithmetic: 6.74 us -> 1.21 us  [on_device(): jnp.where((position >= C - 1)[:, None], context, jnp.zeros_like(context))]
  transfers between devices with their start and end apart: 24 -> 16, of which waited for: 10 -> 5; matrix products, arithmetic and copies ran while one was open for 31% -> 13% of each run, Pallas kernels for 24% -> 24%
where the time goes in v1:
time: 166 us; the launch traced here: 165 us
  Pallas kernels  80.3 us (48%)
  waiting for transfers between devices  21.2 us (13%)
  starting transfers between devices  20.3 us (12%)
  other arithmetic  14.2 us (9%)
  local copies, waits for them, and re-layouts  12 us (7%)
  between operations  10 us (6%)
  matrix products  7.23 us (4%)
    pallas_call x1, Pallas kernels, gather_weights(): pl.pallas_call(gather_kernel, out_shape=[out, out], in_specs=[anywhere] *...  29.8 us
    pallas_call x2, Pallas kernels, one_call(): pl.pallas_call(kernel, out_shape=outs, in_specs=[vmem] * len(args), out_s...  25 us
    pallas_call x1, Pallas kernels, decode(): pl.pallas_call(decode_kernel, grid=(width // (HEADS_STEP * HD),), out_sha...  13.1 us
    pallas_call x4, Pallas kernels, project(): pl.pallas_call(project_kernel, out_shape=jax.ShapeDtypeStruct((tokens, wi...  12.5 us
    ppermute x3, waiting for transfers between devices, on_device(): lax.ppermute(held[:, step], 'seq', moved).astype(jnp.float32)  11.7 us
    ppermute x12, starting transfers between devices, swap(): return lax.ppermute(value, axis, [(i, i ^ distance) for i in range(count)])  10.2 us
    unnamed x34, local copies, waits for them, and re-layouts  8.95 us
    dot_general x1, matrix products, matmul(): return jnp.dot(former, latter, preferred_element_type=jnp.float32)  7.23 us
  transfers between devices with their start and end apart: 16, of which 5 were waited for; matrix products, arithmetic and copies ran while one was open for 13% of the time, Pallas kernels for 24%

profile of v1, /device:TPU:0, one launch (start us, length us, event | category | flops | bytes accessed | tf_op | source)
XLA Modules:
  0.0 165.2 jit_solution(13031785732048210497)
XLA Ops:
  0.6 0.7 reshape.249.gain_ref
  1.3 1.0 copy-done
  2.3 1.0 copy-done.1
  3.3 1.0 copy-done.2
  4.3 1.0 copy-done.3
  5.3 29.8 %shard_map.181 = (bf16[2,896,896]{2,1,0:T(8,128)(2,1)}, bf16[2,896,896]{2,1,0:T(8,128)(2,1)}) custom-call(bf16[224,896]{1,0:T(8,128)(2,1)S(1)} %copy-done, bf16[224,896]{1,0:T(8,128)(2,1)S(1)} %copy-done.1, bf16[224,896]{1,0:T(8,128)(2,1)S(1)} %copy-done.2, bf16[224,896]{1,0:T(8,128)(2,1)S(1)} %copy-done.3), custom_call_target="tpu_custom_call" | custom-call | tf_op jit(solution)/shard_map/pallas_call | solution.py:299
  35.2 7.5 %shard_map.182 = (bf16[256,896]{1,0:T(8,128)(2,1)S(1)}, bf16[256,896]{1,0:T(8,128)(2,1)S(1)}, bf16[256,896]{1,0:T(8,128)(2,1)S(1)}, bf16[256,896]{1,0:T(8,128)(2...) custom-call(bf16[256,896]{1,0:T(8,128)(2,1)} %bitcast.47, ...), custom_call_target="tpu_custom_call" | custom-call | flops 2466250752 | bytes 11472384 | tf_op jit(solution)/shard_map/pallas_call | solution.py:217
  42.6 0.8 copy-done.6
  43.4 0.8 copy-done.8
  44.2 0.4 collective-permute-start.2
  44.5 1.3 collective-permute-start.3
  45.9 0.2 collective-permute-start.4
  46.1 1.5 fusion.3.order_a_ref
  47.6 1.5 fusion.4.order_b_ref
  49.1 17.5 %shard_map.183 = (bf16[256,896]{1,0:T(8,128)(2,1)}, bf16[2,448,896]{2,1,0:T(8,128)(2,1)}, bf16[2,448,896]{2,1,0:T(8,128)(2,1)}, bf16[2,448,896]{2,1,0:T(8,128)(2,1)}, bf16[2,448,896]{2,1,0:T(8,128)(2,1)}) custom-call(bf16[256,896]{1,0:T(8,128)(2,1)S(1)} %bitcast.48, f32[1,896]{1,0:T(1,128)S(1)} %reshape.249.gain_ref, bf16[256,896]{1,0:T(8,128)(2,1)S(1)} %bitcast.49, ...), custom_call_target="tpu_custom_call" | custom-call | flops 5754585088 | bytes 21564928 | tf_op jit(solution)/shard_map/pallas_call | solution.py:217
  66.6 0.7 collective-permute-start
  67.3 0.1 collective-permute-start.1
  67.4 0.5 fusion
  67.9 0.1 pad.6.clone
  68.0 0.6 fusion.2
  68.6 7.2 %fusion.9.q_ref = bf16[320,1024]{1,0:T(8,128)(2,1)} fusion(bf16[4096,1024]{1,0:T(8,128)(2,1)} %param.16, bf16[256,4096]{1,0:T(8,128)(2,1)S(1)} %fusion.2, bf16[320]{0:T(512)(128)(2,1)S(1)} %pad.6.clone, bf16[320]{0:T(512)(128)(2,1)S(1)} %pad.4.clone), kind=kOutput, calls=%fused_computation.17 | convolution fusion | flops 2692546560 | bytes 11142400 | tf_op jit(solution)/shard_map/dot_general | solution.py:28
  75.9 0.6 fusion.41
  85.6 0.1 pad_add_fusion
  85.6 0.1 copy.33.place_ref
  85.8 0.1 select_select_fusion
  85.9 0.1 select_select_fusion.1
  86.0 3.4 %collective-permute-start.5 = (bf16[256,896]{1,0:T(8,128)(2,1)S(1)}, bf16[256,896]{1,0:T(8,128)(2,1)S(1)}, u32[]{:S(2)}, u32[]{:S(2)}) collective-permute-start(bf16[256,896]{1,0:T(8,128)(2,1)S(1)} %pad_maximum_fusion.1), channel_id=1, source_target_pairs={{0,1},{1,2},{2,3},{3,4},{4,5},{5,6},{6,7},{8,9},{9,10},{10,11},{11... | collective-permute-start | bytes 1376264 | tf_op jit(solution)/shard_map/ppermute | solution.py:24
  89.5 1.8 %add_convert_fusion.1 = (bf16[2,224,896]{2,1,0:T(8,128)(2,1)S(1)}, bf16[2,224,896]{2,1,0:T(8,128)(2,1)S(1)}) fusion(bf16[2,448,896]{2,1,0:T(8,128)(2,1)} %collective-permute-done, bf16[2,448,896]{2,1,0:T(8,128)(2,1)S(1)} %copy-done.11), kind=kLoop, calls=%fused_computation.14 | loop fusion | flops 3211264 | bytes 4816896 | tf_op jit(solution)/shard_map/convert_element_type | solution.py:419
  91.3 0.4 add_convert_fusion
  91.7 0.6 collective-permute-start.6
  92.3 2.5 %collective-permute-start.7 = (bf16[2,224,896]{2,1,0:T(8,128)(2,1)S(1)}, bf16[2,224,896]{2,1,0:T(8,128)(2,1)S(1)}, u32[]{:S(2)}, u32[]{:S(2)}) collective-permute-start(bf16[2,224,896]{2,1,0:T(8,128)(2,1)S(1)} %get-tuple-element.58), channel_id=1, source_target_pairs={{0,1},{1,0},{2,3},{3,2},{4,5},{5,4},{6,7},{7,6},{8,9},{9,8},{10,11... | collective-permute-start | bytes 2408456 | tf_op jit(solution)/shard_map/ppermute | solution.py:230
  94.8 5.5 %collective-permute-done.5.refs_4_ = bf16[256,896]{1,0:T(8,128)(2,1)S(1)} collective-permute-done((bf16[256,896]{1,0:T(8,128)(2,1)S(1)}, bf16[256,896]{1,0:T(8,128)(2,1)S(1)}, u32[]{:S(2)}, u32[]{:S(2)}) %collective-permute-start.5) | collective-permute-done | bytes 458784 | tf_op jit(solution)/shard_map/ppermute | solution.py:24
  100.2 0.8 copy-done.14
  101.0 13.1 %shard_map.184 = bf16[320,1024]{1,0:T(8,128)(2,1)} custom-call(s32[5,2]{1,0:T(8,128)S(1)} %copy.33.place_ref, bf16[320,1024]{1,0:T(8,128)(2,1)} %fusion.9.q_ref, bf16[896,1024]{1,0:T(8,128)(2,1)} %wk_ref.1, bf16[896,1024]{1,0:T(8,128)(2,1)} %wv_ref.1, bf16[256,896]{1,0:T(8,128)(2,1)S(1)} %get-tuple-element.53.refs_0_, ...), custom_call_target="tpu_custom_call" | custom-call | flops 10066329600 | bytes 5963776 | tf_op jit(solution)/shard_map/pallas_call | solution.py:194
  114.1 1.2 slice_select_fusion.context_ref
  115.3 0.2 add_convert_fusion.9
  115.5 1.5 collective-permute-done.7
  117.0 0.9 add_convert_fusion.8
  117.9 3.1 %shard_map.186 = bf16[256,1024]{1,0:T(8,128)(2,1)S(1)} custom-call(s32[1]{0:T(128)} %bitcast.18._, bf16[256,1024]{1,0:T(8,128)(2,1)S(1)} %slice_select_fusion.context_ref, bf16[1024,4096]{1,0:T(8,128)(2,1)} %weight_ref.7), custom_call_target="tpu_custom_call" | custom-call | flops 536870912 | bytes 2097152 | tf_op jit(solution)/shard_map/pallas_call | solution.py:324
  121.1 0.6 collective-permute-start.12
  121.7 2.5 %collective-permute-start.11 = (bf16[2,112,896]{2,1,0:T(8,128)(2,1)S(1)}, bf16[2,112,896]{2,1,0:T(8,128)(2,1)S(1)}, u32[]{:S(2)}, u32[]{:S(2)}) collective-permute-start(bf16[2,112,896]{2,1,0:T(8,128)(2,1)S(1)} %get-tuple-element.65), channel_id=1, source_target_pairs={{0,1},{1,0},{2,3},{3,2},{4,5},{5,4},{6,7},{7,6},{8,9},{9,8},{10,11... | collective-permute-start | bytes 1204232 | tf_op jit(solution)/shard_map/ppermute | solution.py:230
  124.2 3.1 %shard_map.185 = bf16[256,1024]{1,0:T(8,128)(2,1)S(1)} custom-call(s32[1]{0:T(128)} %bitcast.17._, bf16[256,1024]{1,0:T(8,128)(2,1)S(1)} %slice_select_fusion.context_ref, bf16[1024,4096]{1,0:T(8,128)(2,1)} %weight_ref.7), custom_call_target="tpu_custom_call" | custom-call | flops 536870912 | bytes 2097152 | tf_op jit(solution)/shard_map/pallas_call | solution.py:324
  127.3 0.2 add_convert_fusion.5
  127.5 3.1 %shard_map.187 = bf16[256,1024]{1,0:T(8,128)(2,1)S(1)} custom-call(s32[1]{0:T(128)} %bitcast.2._, bf16[256,1024]{1,0:T(8,128)(2,1)S(1)} %slice_select_fusion.context_ref, bf16[1024,4096]{1,0:T(8,128)(2,1)} %weight_ref.7), custom_call_target="tpu_custom_call" | custom-call | flops 536870912 | bytes 2097152 | tf_op jit(solution)/shard_map/pallas_call | solution.py:324
  130.7 2.5 %collective-permute-done.12 = bf16[2,112,896]{2,1,0:T(8,128)(2,1)} collective-permute-done((bf16[2,112,896]{2,1,0:T(8,128)(2,1)}, bf16[2,112,896]{2,1,0:T(8,128)(2,1)}, u32[]{:S(2)}, u32[]{:S(2)}) %collective-permute-start.12) | collective-permute-done | bytes 401440 | tf_op jit(solution)/shard_map/ppermute | solution.py:230
  133.2 1.1 add_convert_fusion.6
  134.3 0.1 add_convert_fusion.7
  134.4 0.1 pad_maximum_fusion
  134.5 0.3 copy.34
  134.8 1.0 slice_bitcast_fusion.2
  135.8 5.6 %collective-permute-start.15 = (bf16[4,28,896]{2,0,1:T(4,128)(2,1)}, bf16[4,28,896]{2,0,1:T(4,128)(2,1)}, u32[]{:S(2)}, u32[]{:S(2)}) collective-permute-start(bf16[4,28,896]{2,0,1:T(4,128)(2,1)} %get-tuple-element.77), channel_id=1, source_target_pairs={{0,6},{1,7},{2,0},{3,1},{4,2},{5,3},{6,4},{7,5},{8,14},{9,15},{10,... | collective-permute-start | bytes 602120 | tf_op jit(solution)/shard_map/ppermute | solution.py:494
  141.4 1.0 collective-permute-start.13
  142.4 1.3 collective-permute-start.10
  143.7 3.1 %shard_map.188 = bf16[256,1024]{1,0:T(8,128)(2,1)S(1)} custom-call(s32[1]{0:T(128)} %bitcast.19._, bf16[256,1024]{1,0:T(8,128)(2,1)S(1)} %slice_select_fusion.context_ref, bf16[1024,4096]{1,0:T(8,128)(2,1)} %weight_ref.7), custom_call_target="tpu_custom_call" | custom-call | flops 536870912 | bytes 2097152 | tf_op jit(solution)/shard_map/pallas_call | solution.py:324
  146.8 0.1 collective-permute-start.9
  146.9 0.2 collective-permute-done.15
  147.2 11.4 %collective-permute-done.14 = bf16[4,28,896]{2,0,1:T(4,128)(2,1)} collective-permute-done((bf16[4,28,896]{2,0,1:T(4,128)(2,1)}, bf16[4,28,896]{2,0,1:T(4,128)(2,1)}, u32[]{:S(2)}, u32[]{:S(2)}) %collective-permute-start.14) | collective-permute-done | bytes 200736 | tf_op jit(solution)/shard_map/ppermute | solution.py:494
  158.6 1.3 fusion.16
  159.9 0.3 fusion.40
  160.2 0.7 copy.46
  160.9 0.7 copy.45
  161.5 0.7 copy.44
  162.2 0.7 copy.43
  162.8 2.3 %add_convert_fusion.4 = bf16[256,1024]{1,0:T(8,128)(2,1)} fusion(bf16[256,1024]{1,0:T(8,128)(2,1)S(1)} %collective-permute-done.10, bf16[256,1024]{1,0:T(8,128)(2,1)} %collective-permute-done.9, bf16[256,1024]{1,0:T(8,128)(2,1)S(1)} %shard_map.187, bf16[256,4096]{1,0:T(8,128)(2,1)} %param.14, s32[]{:T(128)S(6)} %select_n.272), kind=kLoop, calls=%fused_computation.20 | loop fusion | flops 2097152 | bytes 2621444 | tf_op jit(solution)/shard_map/convert_element_type | solution.py:500
  (44 shorter events, 0.3 us)
Async XLA Ops:
  1.3 1.0 copy-start
  2.3 1.0 copy-start.1
  3.3 1.0 copy-start.2
  4.3 1.0 copy-start.3
  42.6 0.8 copy-start.6
  43.4 0.8 copy-start.8
  44.2 4.9 %copy-start.4 = (bf16[1,2,128,896]{3,2,1,0:T(8,128)(2,1)S(1)}, bf16[1,2,128,896]{3,2,1,0:T(8,128)(2,1)}, u32[]{:S(2)}) copy-start(bf16[1,2,128,896]{3,2,1,0:T(8,128)(2,1)} %param.20) | copy-start | bytes 1376260
  44.2 4.9 %copy-start.5 = (bf16[1,2,128,896]{3,2,1,0:T(8,128)(2,1)S(1)}, bf16[1,2,128,896]{3,2,1,0:T(8,128)(2,1)}, u32[]{:S(2)}) copy-start(bf16[1,2,128,896]{3,2,1,0:T(8,128)(2,1)} %param.26) | copy-start | bytes 1376260
  44.2 41.6 %collective-permute-start.2 = (bf16[256,896]{1,0:T(8,128)(2,1)S(1)}, bf16[256,896]{1,0:T(8,128)(2,1)S(1)}, u32[]{:S(2)}, u32[]{:S(2)}) collective-permute-start(bf16[256,896]{1,0:T(8,128)(2,1)S(1)} %get-tuple-element.53.refs_0_), channel_id=1, source_target_pairs={{0,8},{8,0},{16,24},{24,16},{1,9},{9,1},{17,25},{25,17},{2,10},{10... | collective-permute-start | bytes 1376264 | tf_op jit(solution)/shard_map/ppermute | solution.py:230
  44.5 41.2 %collective-permute-start.3 = (bf16[256,896]{1,0:T(8,128)(2,1)S(1)}, bf16[256,896]{1,0:T(8,128)(2,1)S(1)}, u32[]{:S(2)}, u32[]{:S(2)}) collective-permute-start(bf16[256,896]{1,0:T(8,128)(2,1)S(1)} %get-tuple-element.53.refs_0_), channel_id=1, source_target_pairs={{0,16},{8,24},{16,0},{24,8},{1,17},{9,25},{17,1},{25,9},{2,18},{10... | collective-permute-start | bytes 1376264 | tf_op jit(solution)/shard_map/ppermute | solution.py:230
  45.9 39.9 %collective-permute-start.4 = (bf16[256,896]{1,0:T(8,128)(2,1)S(1)}, bf16[256,896]{1,0:T(8,128)(2,1)S(1)}, u32[]{:S(2)}, u32[]{:S(2)}) collective-permute-start(bf16[256,896]{1,0:T(8,128)(2,1)S(1)} %get-tuple-element.53.refs_0_), channel_id=1, source_target_pairs={{0,24},{8,16},{16,8},{24,0},{1,25},{9,17},{17,9},{25,1},{2,26},{10... | collective-permute-start | bytes 1376264 | tf_op jit(solution)/shard_map/ppermute | solution.py:230
  46.0 3.1 %copy-start.7 = (bf16[256,896]{1,0:T(8,128)(2,1)S(1)}, bf16[256,896]{1,0:T(8,128)(2,1)}, u32[]{:S(2)}) copy-start(bf16[256,896]{1,0:T(8,128)(2,1)} %copy-done.6) | copy-start | bytes 1376260
  49.1 18.3 %copy-start.9 = (bf16[256,4096]{1,0:T(8,128)(2,1)S(1)}, bf16[256,4096]{1,0:T(8,128)(2,1)}, u32[]{:S(2)}) copy-start(bf16[256,4096]{1,0:T(8,128)(2,1)} %param.14) | copy-start | bytes 6291460
  66.6 1.4 copy-start.12
  66.6 22.9 %collective-permute-start = (bf16[2,448,896]{2,1,0:T(8,128)(2,1)}, bf16[2,448,896]{2,1,0:T(8,128)(2,1)}, u32[]{:S(2)}, u32[]{:S(2)}) collective-permute-start(bf16[2,448,896]{2,1,0:T(8,128)(2,1)} %get-tuple-element.49), channel_id=1, source_target_pairs={{0,8},{8,0},{16,24},{24,16},{1,9},{9,1},{17,25},{25,17},{2,10},{10... | collective-permute-start | bytes 4816904 | tf_op jit(solution)/shard_map/ppermute | solution.py:230
  67.3 24.0 %collective-permute-start.1 = (bf16[2,448,896]{2,1,0:T(8,128)(2,1)}, bf16[2,448,896]{2,1,0:T(8,128)(2,1)S(1)}, u32[]{:S(2)}, u32[]{:S(2)}) collective-permute-start(bf16[2,448,896]{2,1,0:T(8,128)(2,1)} %get-tuple-element.51), channel_id=1, source_target_pairs={{0,8},{8,0},{16,24},{24,16},{1,9},{9,1},{17,25},{25,17},{2,10},{10... | collective-permute-start | bytes 4816904 | tf_op jit(solution)/shard_map/ppermute | solution.py:230
  68.6 7.2 %copy-start.13 = (s32[4,2]{0,1:T(2,128)S(1)}, s32[4,2]{0,1:T(2,128)}, u32[]{:S(2)}) copy-start(s32[4,2]{0,1:T(2,128)} %param.27) | copy-start | bytes 100
  85.8 3.7 %copy-start.11 = (bf16[2,448,896]{2,1,0:T(8,128)(2,1)S(1)}, bf16[2,448,896]{2,1,0:T(8,128)(2,1)}, u32[]{:S(2)}) copy-start(bf16[2,448,896]{2,1,0:T(8,128)(2,1)} %get-tuple-element.48) | copy-start | bytes 4816900
  86.0 5.3 %copy-start.10 = (bf16[2,448,896]{2,1,0:T(8,128)(2,1)S(1)}, bf16[2,448,896]{2,1,0:T(8,128)(2,1)}, u32[]{:S(2)}) copy-start(bf16[2,448,896]{2,1,0:T(8,128)(2,1)} %get-tuple-element.50) | copy-start | bytes 4816900
  86.0 14.2 %collective-permute-start.5 = (bf16[256,896]{1,0:T(8,128)(2,1)S(1)}, bf16[256,896]{1,0:T(8,128)(2,1)S(1)}, u32[]{:S(2)}, u32[]{:S(2)}) collective-permute-start(bf16[256,896]{1,0:T(8,128)(2,1)S(1)} %pad_maximum_fusion.1), channel_id=1, source_target_pairs={{0,1},{1,2},{2,3},{3,4},{4,5},{5,6},{6,7},{8,9},{9,10},{10,11},{11... | collective-permute-start | bytes 1376264 | tf_op jit(solution)/shard_map/ppermute | solution.py:24
  91.7 23.6 %collective-permute-start.6 = (bf16[2,224,896]{2,1,0:T(8,128)(2,1)S(1)}, bf16[2,224,896]{2,1,0:T(8,128)(2,1)S(1)}, u32[]{:S(2)}, u32[]{:S(2)}) collective-permute-start(bf16[2,224,896]{2,1,0:T(8,128)(2,1)S(1)} %get-tuple-element.56), channel_id=1, source_target_pairs={{0,16},{8,24},{16,0},{24,8},{1,17},{9,25},{17,1},{25,9},{2,18},{10... | collective-permute-start | bytes 2408456 | tf_op jit(solution)/shard_map/ppermute | solution.py:230
  92.3 24.7 %collective-permute-start.7 = (bf16[2,224,896]{2,1,0:T(8,128)(2,1)S(1)}, bf16[2,224,896]{2,1,0:T(8,128)(2,1)S(1)}, u32[]{:S(2)}, u32[]{:S(2)}) collective-permute-start(bf16[2,224,896]{2,1,0:T(8,128)(2,1)S(1)} %get-tuple-element.58), channel_id=1, source_target_pairs={{0,1},{1,0},{2,3},{3,2},{4,5},{5,4},{6,7},{7,6},{8,9},{9,8},{10,11... | collective-permute-start | bytes 2408456 | tf_op jit(solution)/shard_map/ppermute | solution.py:230
  100.2 0.8 copy-start.14
  121.1 6.3 %collective-permute-start.8 = (bf16[256,1024]{1,0:T(8,128)(2,1)S(1)}, bf16[256,1024]{1,0:T(8,128)(2,1)S(1)}, u32[]{:S(2)}, u32[]{:S(2)}) collective-permute-start(bf16[256,1024]{1,0:T(8,128)(2,1)S(1)} %shard_map.186), channel_id=1, source_target_pairs={{0,8},{8,0},{16,24},{24,16},{1,9},{9,1},{17,25},{25,17},{2,10},{10... | collective-permute-start | bytes 1572872 | tf_op jit(solution)/shard_map/ppermute | solution.py:230
  121.1 12.0 %collective-permute-start.12 = (bf16[2,112,896]{2,1,0:T(8,128)(2,1)}, bf16[2,112,896]{2,1,0:T(8,128)(2,1)}, u32[]{:S(2)}, u32[]{:S(2)}) collective-permute-start(bf16[2,112,896]{2,1,0:T(8,128)(2,1)} %get-tuple-element.67), channel_id=1, source_target_pairs={{0,16},{8,24},{16,0},{24,8},{1,17},{9,25},{17,1},{25,9},{2,18},{10... | collective-permute-start | bytes 1204232 | tf_op jit(solution)/shard_map/ppermute | solution.py:230
  121.7 12.5 %collective-permute-start.11 = (bf16[2,112,896]{2,1,0:T(8,128)(2,1)S(1)}, bf16[2,112,896]{2,1,0:T(8,128)(2,1)S(1)}, u32[]{:S(2)}, u32[]{:S(2)}) collective-permute-start(bf16[2,112,896]{2,1,0:T(8,128)(2,1)S(1)} %get-tuple-element.65), channel_id=1, source_target_pairs={{0,1},{1,0},{2,3},{3,2},{4,5},{5,4},{6,7},{7,6},{8,9},{9,8},{10,11... | collective-permute-start | bytes 1204232 | tf_op jit(solution)/shard_map/ppermute | solution.py:230
  135.8 11.4 %collective-permute-start.15 = (bf16[4,28,896]{2,0,1:T(4,128)(2,1)}, bf16[4,28,896]{2,0,1:T(4,128)(2,1)}, u32[]{:S(2)}, u32[]{:S(2)}) collective-permute-start(bf16[4,28,896]{2,0,1:T(4,128)(2,1)} %get-tuple-element.77), channel_id=1, source_target_pairs={{0,6},{1,7},{2,0},{3,1},{4,2},{5,3},{6,4},{7,5},{8,14},{9,15},{10,... | collective-permute-start | bytes 602120 | tf_op jit(solution)/shard_map/ppermute | solution.py:494
  141.4 17.2 %collective-permute-start.14 = (bf16[4,28,896]{2,0,1:T(4,128)(2,1)}, bf16[4,28,896]{2,0,1:T(4,128)(2,1)}, u32[]{:S(2)}, u32[]{:S(2)}) collective-permute-start(bf16[4,28,896]{2,0,1:T(4,128)(2,1)} %get-tuple-element.78), channel_id=1, source_target_pairs={{0,4},{1,5},{2,6},{3,7},{4,0},{5,1},{6,2},{7,3},{8,12},{9,13},{10,... | collective-permute-start | bytes 602120 | tf_op jit(solution)/shard_map/ppermute | solution.py:494
  141.4 17.2 %collective-permute-start.13 = (bf16[4,28,896]{2,0,1:T(4,128)(2,1)}, bf16[4,28,896]{2,0,1:T(4,128)(2,1)}, u32[]{:S(2)}, u32[]{:S(2)}) collective-permute-start(bf16[4,28,896]{2,0,1:T(4,128)(2,1)} %get-tuple-element.76), channel_id=1, source_target_pairs={{0,2},{1,3},{2,4},{3,5},{4,6},{5,7},{6,0},{7,1},{8,10},{9,11},{10,... | collective-permute-start | bytes 602120 | tf_op jit(solution)/shard_map/ppermute | solution.py:494
  142.4 20.4 %collective-permute-start.10 = (bf16[256,1024]{1,0:T(8,128)(2,1)S(1)}, bf16[256,1024]{1,0:T(8,128)(2,1)S(1)}, u32[]{:S(2)}, u32[]{:S(2)}) collective-permute-start(bf16[256,1024]{1,0:T(8,128)(2,1)S(1)} %add_convert_fusion.5), channel_id=1, source_target_pairs={{0,16},{8,24},{16,0},{24,8},{1,17},{9,25},{17,1},{25,9},{2,18},{10... | collective-permute-start | bytes 1572872 | tf_op jit(solution)/shard_map/ppermute | solution.py:230
  146.8 16.0 %collective-permute-start.9 = (bf16[256,1024]{1,0:T(8,128)(2,1)S(1)}, bf16[256,1024]{1,0:T(8,128)(2,1)}, u32[]{:S(2)}, u32[]{:S(2)}) collective-permute-start(bf16[256,1024]{1,0:T(8,128)(2,1)S(1)} %shard_map.188), channel_id=1, source_target_pairs={{0,8},{8,0},{16,24},{24,16},{1,9},{9,1},{17,25},{25,17},{2,10},{10... | collective-permute-start | bytes 1572872 | tf_op jit(solution)/shard_map/ppermute | solution.py:230

commit v2 on v1

--- a/solution.py
+++ b/solution.py
@@ -1,3 +1,5 @@
+import functools
+
 import jax
 import jax.numpy as jnp
 from jax import lax
@@ -182,7 +184,8 @@
             ctx_ref[group * C : (group + 1) * C, lanes] = total.astype(jnp.bfloat16)
 
 
-LIMIT = 52 * 1024 * 1024
+LIMIT = 60 * 1024 * 1024
+SMALL_LIMIT = 24 * 1024 * 1024
 
 
 def decode(place, queries, key_weight, value_weight, pieces):
@@ -204,7 +207,7 @@
         + whole,
         out_specs=pl.BlockSpec((count, HEADS_STEP * HD), column),
         scratch_shapes=[pltpu.VMEM((rows, 2 * HEADS_STEP * HD), jnp.bfloat16)],
-        compiler_params=pltpu.CompilerParams(vmem_limit_bytes=LIMIT),
+        compiler_params=pltpu.CompilerParams(vmem_limit_bytes=SMALL_LIMIT),
         cost_estimate=pl.CostEstimate(
             flops=2 * flops, bytes_accessed=rows * DE * 2 + 4 * DE * width, transcendentals=0
         ),
@@ -295,7 +298,7 @@
 def gather_weights(blocks, count):
     height, width = blocks[0].shape
     out = jax.ShapeDtypeStruct((2, count * height, width), blocks[0].dtype)
-    anywhere = pl.BlockSpec(memory_space=pl.ANY)
+    anywhere = pl.BlockSpec(memory_space=pltpu.HBM)
     return pl.pallas_call(
         gather_kernel,
         out_shape=[out, out],
@@ -312,6 +315,73 @@
     )(*blocks)
 
 
+def choose_kernel(place_ref, *refs):
+    pieces, out_ref = refs[:-1], refs[-1]
+    tiles = pieces[0].shape[0] // R
+    for at in range(K):
+        for i in range(len(pieces) * tiles):
+
+            @pl.when(place_ref[place_ref.shape[0] - 1, at] == i)
+            def _():
+                start = i % tiles * R
+                out_ref[at * R : (at + 1) * R, :] = pieces[i // tiles][start : start + R, :]
+
+
+def choose(place, pieces):
+    vmem = pl.BlockSpec(memory_space=pltpu.VMEM)
+    return pl.pallas_call(
+        choose_kernel,
+        out_shape=jax.ShapeDtypeStruct((K * R, pieces[0].shape[1]), pieces[0].dtype),
+        in_specs=[pl.BlockSpec(memory_space=pltpu.SMEM)] + [vmem] * len(pieces),
+        out_specs=vmem,
+        compiler_params=pltpu.CompilerParams(vmem_limit_bytes=SMALL_LIMIT),
+    )(place, *pieces)
+
+
+def shares_kernel(a_keep, a_came, b_keep, b_came, *outs):
+    rows = outs[0].shape[1]
+    for pair, (keep, came) in enumerate(((a_keep, a_came), (b_keep, b_came))):
+        for which in range(2):
+            total = keep[which].astype(jnp.float32) + came[which].astype(jnp.float32)
+            for at, out_ref in enumerate(outs):
+                out_ref[2 * pair + which] = total[at * rows : (at + 1) * rows].astype(
+                    jnp.bfloat16
+                )
+
+
+def shares(a_keep, a_came, b_keep, b_came, count):
+    vmem = pl.BlockSpec(memory_space=pltpu.VMEM)
+    _, rows, width = a_keep.shape
+    out = jax.ShapeDtypeStruct((4, rows // count, width), jnp.bfloat16)
+    return pl.pallas_call(
+        shares_kernel,
+        out_shape=[out] * count,
+        in_specs=[vmem] * 4,
+        out_specs=[vmem] * count,
+        compiler_params=pltpu.CompilerParams(vmem_limit_bytes=SMALL_LIMIT),
+    )(a_keep, a_came, b_keep, b_came)
+
+
+def finish_kernel(scale, *refs):
+    parts, outs = refs[:-4], refs[-4:]
+    for which, out_ref in enumerate(outs):
+        total = parts[0][which].astype(jnp.float32)
+        for part in parts[1:]:
+            total = total + part[which].astype(jnp.float32)
+        out_ref[...] = total * scale
+
+
+def finish(parts, scale):
+    vmem = pl.BlockSpec(memory_space=pltpu.VMEM)
+    return pl.pallas_call(
+        functools.partial(finish_kernel, scale),
+        out_shape=[jax.ShapeDtypeStruct(parts[0].shape[1:], jnp.float32)] * 4,
+        in_specs=[vmem] * len(parts),
+        out_specs=[vmem] * 4,
+        compiler_params=pltpu.CompilerParams(vmem_limit_bytes=SMALL_LIMIT),
+    )(*parts)
+
+
 def project_kernel(_, context_ref, weight_ref, out_ref):
     out_ref[...] = matmul(context_ref[...], weight_ref[...]).astype(jnp.bfloat16)
 
@@ -319,7 +389,7 @@
 def project(context, weight, which, count):
     tokens, depth = context.shape
     width = weight.shape[1] // count
-    steps = 4
+    steps = 2
     tile = width // steps
     return pl.pallas_call(
         project_kernel,
@@ -333,7 +403,7 @@
             ],
             out_specs=pl.BlockSpec((tokens, tile), lambda i, at: (0, i)),
         ),
-        compiler_params=pltpu.CompilerParams(vmem_limit_bytes=LIMIT),
+        compiler_params=pltpu.CompilerParams(vmem_limit_bytes=SMALL_LIMIT),
         cost_estimate=pl.CostEstimate(
             flops=2 * tokens * depth * width, bytes_accessed=2 * depth * width, transcendentals=0
         ),
@@ -423,10 +493,6 @@
         return added(keep[:, :half], came[:, :half]), added(keep[:, half:], came[:, half:])
 
     came_a, came_b = swap(a_send, "enc", 1), swap(b_send, "enc", 1)
-    hidden, a_keep, b_keep = lax.optimization_barrier((hidden, a_keep, b_keep))
-    a_keep, a_send = cut(a_keep, came_a)
-    b_keep, b_send = cut(b_keep, came_b)
-
     sibling = swap(encoded, "enc", 1)
     across = swap(encoded, "enc", 2)
     across_sibling = swap(encoded, "enc", 3)
@@ -434,15 +500,9 @@
     owner = neighbour_ids // local_count
     place = (owner ^ enc_at) * local_count + neighbour_ids % local_count
     stretch_count = neighbour_ids.shape[0]
-    tokens = [piece.reshape(local_count, R, DE) for piece in pieces]
-
-    def chosen(at):
-        value = tokens[0][0]
-        for i in range(1, enc_count * local_count):
-            value = jnp.where(at == i, tokens[i // local_count][i % local_count], value)
-        return value
-
-    last = jnp.concatenate([chosen(place[stretch_count - 1, i]) for i in range(K)], axis=0)
+    place = place.astype(jnp.int32)
+    last = choose(place, pieces)
+    hidden, a_keep, b_keep, last = lax.optimization_barrier((hidden, a_keep, b_keep, last))
     earlier_rows = shifted(last, "seq", 1)
     hidden_f = hidden.astype(jnp.float32)
     inv_rms = lax.rsqrt(jnp.mean(hidden_f * hidden_f, axis=-1, keepdims=True) + EPS)
@@ -457,11 +517,14 @@
         axis=0,
     )
     queries = matmul(padded, cca_query).astype(jnp.bfloat16)
+    queries, a_keep, b_keep = lax.optimization_barrier((queries, a_keep, b_keep))
+    a_keep, a_send = cut(a_keep, came_a)
+    b_keep, b_send = cut(b_keep, came_b)
     queries, a_send, b_send = lax.optimization_barrier((queries, a_send, b_send))
     came_a, came_b = swap(a_send, "enc", 2), swap(b_send, "seq", 1)
     pool_count = enc_count * local_count
     in_order = pool_count + jnp.arange(K, dtype=jnp.int32).reshape(1, K)
-    spots = jnp.concatenate([in_order, place.astype(jnp.int32)], axis=0)
+    spots = jnp.concatenate([in_order, place], axis=0)
     context = decode(spots, queries, cca_key, cca_value, (*pieces, earlier_rows))
     context, a_keep, b_keep = lax.optimization_barrier((context, a_keep, b_keep))
     a_keep, a_send = cut(a_keep, came_a)
@@ -485,14 +548,12 @@
     near_sent = swap(column(context, 1), "enc", 1)
     near = column(context, 0)
     near, a_keep, b_keep = lax.optimization_barrier((near, a_keep, b_keep))
-    held = jnp.concatenate([added(a_keep, came_a), added(b_keep, came_b)], axis=0).reshape(
-        4, lines, own_rows, DE
-    )
-    total = held[:, 0].astype(jnp.float32)
+    held = shares(a_keep, came_a, b_keep, came_b, lines)
+    parts = [held[0]]
     for step in range(1, lines):
         moved = [(i, (i + 2 * step) % seq_count) for i in range(seq_count)]
-        total = total + lax.ppermute(held[:, step], "seq", moved).astype(jnp.float32)
-    total = total / (local_count * enc_count * seq_count)
+        parts.append(lax.ppermute(held[step], "seq", moved))
+    total = finish(parts, 1.0 / (local_count * enc_count * seq_count))
     branch = (
         near.astype(jnp.float32) + near_sent.astype(jnp.float32) + landed.astype(jnp.float32)
     )

time: 166 us -> 166 us (level); the launches traced: 165 us -> 164 us
  Pallas kernels: 80.3 us -> 96 us
  between operations: 10 us -> 0.97 us
  local copies, waits for them, and re-layouts: 12 us -> 5.64 us
  waiting for transfers between devices: 21.2 us -> 25.1 us
  other arithmetic: 14.2 us -> 10.5 us
    pallas_call x1, Pallas kernels: 29.8 us -> 53.1 us  [gather_weights(): pl.pallas_call(gather_kernel, out_shape=[out, out], in_specs=[anywhere] *...]
    pallas_call x4, Pallas kernels: 12.5 us -> 4.42 us  [project(): pl.pallas_call(project_kernel, out_shape=jax.ShapeDtypeStruct((tokens, wi...]
    unnamed x34 -> x23, local copies, waits for them, and re-layouts: 8.95 us -> 4.28 us
    ppermute x12, waiting for transfers between devices: 4.03 us -> 6.8 us  [swap(): return lax.ppermute(value, axis, [(i, i ^ distance) for i in range(count)])]
    pallas_call x0 -> x3, Pallas kernels: none -> 1.78 us  [the longest x1 0.81 us: finish(): pl.pallas_call(functools.partial(finish_kernel, scale), out_shape=[jax.Sh...]
    convert_element_type x7 -> x5, other arithmetic: 4.73 us -> 3.57 us  [added(): (former.astype(jnp.float32) + latter.astype(jnp.float32)).astype(jnp.bflo...]
  transfers between devices with their start and end apart: 16 -> 16, of which waited for: 5 -> 5; matrix products, arithmetic and copies ran while one was open for 13% -> 9% of each run, Pallas kernels for 24% -> 21%
where the time goes in v2:
time: 166 us; the launch traced here: 164 us
  Pallas kernels  96 us (58%)
  waiting for transfers between devices  25.1 us (15%)
  starting transfers between devices  18.9 us (11%)
  other arithmetic  10.5 us (6%)
  matrix products  6.47 us (4%)
  local copies, waits for them, and re-layouts  5.64 us (3%)
    pallas_call x1, Pallas kernels, gather_weights(): pl.pallas_call(gather_kernel, out_shape=[out, out], in_specs=[anywhere] *...  53.1 us
    pallas_call x2, Pallas kernels, one_call(): pl.pallas_call(kernel, out_shape=outs, in_specs=[vmem] * len(args), out_s...  24.8 us
    ppermute x3, waiting for transfers between devices, on_device(): parts.append(lax.ppermute(held[step], 'seq', moved))  12.8 us
    pallas_call x1, Pallas kernels, decode(): pl.pallas_call(decode_kernel, grid=(width // (HEADS_STEP * HD),), out_sha...  11.9 us
    ppermute x12, starting transfers between devices, swap(): return lax.ppermute(value, axis, [(i, i ^ distance) for i in range(count)])  10.2 us
    ppermute x12, waiting for transfers between devices, swap(): return lax.ppermute(value, axis, [(i, i ^ distance) for i in range(count)])  6.8 us
    dot_general x1, matrix products, matmul(): return jnp.dot(former, latter, preferred_element_type=jnp.float32)  6.47 us
    ppermute x1, waiting for transfers between devices, shifted(): lax.ppermute(value, axis, [(source, source + steps) for source in range(i...  5.46 us
  transfers between devices with their start and end apart: 16, of which 5 were waited for; matrix products, arithmetic and copies ran while one was open for 9% of the time, Pallas kernels for 21%

profile of v2, /device:TPU:0, one launch (start us, length us, event | category | flops | bytes accessed | tf_op | source)
XLA Modules:
  0.0 163.5 jit_solution(5289301911350636574)
XLA Ops:
  0.6 1.3 reshape.196.gain_ref
  1.9 53.1 %shard_map.181 = (bf16[2,896,896]{2,1,0:T(8,128)(2,1)}, bf16[2,896,896]{2,1,0:T(8,128)(2,1)}) custom-call(bf16[224,896]{1,0:T(8,128)(2,1)} %q_ref.1, bf16[224,896]{1,0:T(8,128)(2,1)} %k_ref.1, bf16[224,896]{1,0:T(8,128)(2,1)} %v_ref.1, bf16[224,896]{1,0:T(8,128)(2,1)} %o_ref.1), custom_call_target="tpu_custom_call" | custom-call | tf_op jit(solution)/shard_map/pallas_call | solution.py:302
  55.0 7.7 %shard_map.182 = (bf16[256,896]{1,0:T(8,128)(2,1)}, bf16[256,896]{1,0:T(8,128)(2,1)}, bf16[256,896]{1,0:T(8,128)(2,1)}, bf16[256,896]{1,0:T(8,128)(2,1)}, bf16[2...) custom-call(bf16[256,896]{1,0:T(8,128)(2,1)} %bitcast.11, f32[1,896]{1,0:T(1,128)} %reshape.196.gain_ref, ...), custom_call_target="tpu_custom_call" | custom-call | flops 2466250752 | bytes 11472384 | tf_op jit(solution)/shard_map/pallas_call | solution.py:220
  62.7 0.0 collective-permute-start
  62.7 1.6 collective-permute-start.1
  64.2 0.3 collective-permute-start.2
  64.6 1.5 fusion.3.order_a_ref
  66.1 1.5 fusion.4.order_b_ref
  67.6 17.1 %shard_map.183 = (bf16[256,896]{1,0:T(8,128)(2,1)}, bf16[2,448,896]{2,1,0:T(8,128)(2,1)}, bf16[2,448,896]{2,1,0:T(8,128)(2,1)}, bf16[2,448,896]{2,1,0:T(8,128)(2,1)}, bf16[2,448,896]{2,1,0:T(8,128)(2,1)}) custom-call(bf16[256,896]{1,0:T(8,128)(2,1)} %bitcast.12, f32[1,896]{1,0:T(1,128)} %reshape.196.gain_ref, bf16[256,896]{1,0:T(8,128)(2,1)} %bitcast.13, ...), custom_call_target="tpu_custom_call" | custom-call | flops 5754585088 | bytes 21564928 | tf_op jit(solution)/shard_map/pallas_call | solution.py:220
  84.7 0.4 collective-permute-start.4
  85.1 0.2 collective-permute-start.3
  85.3 0.1 copy.30
  85.4 0.1 pad.2.clone
  85.5 0.0 copy-start.7
  85.5 0.0 collective-permute-done.refs_1_
  85.5 0.0 collective-permute-done.1.refs_2_
  85.5 0.0 collective-permute-done.2.refs_3_
  85.5 0.7 shard_map.184
  86.3 0.8 copy-done.4
  87.0 0.5 fusion
  87.5 0.6 fusion.2
  88.2 6.5 %fusion.9.q_ref = bf16[320,1024]{1,0:T(8,128)(2,1)S(1)} fusion(bf16[4096,1024]{1,0:T(8,128)(2,1)} %param.16, bf16[256,4096]{1,0:T(8,128)(2,1)S(1)} %fusion.2, bf16[320]{0:T(512)(128)(2,1)S(1)} %pad.2.clone, bf16[320]{0:T(512)(128)(2,1)S(1)} %pad.clone), kind=kOutput, calls=%fused_computation.17 | convolution fusion | flops 2692546560 | bytes 11142400 | tf_op jit(solution)/shard_map/dot_general | solution.py:30
  94.7 3.6 %collective-permute-start.5 = (bf16[256,896]{1,0:T(8,128)(2,1)S(1)}, bf16[256,896]{1,0:T(8,128)(2,1)S(1)}, u32[]{:S(2)}, u32[]{:S(2)}) collective-permute-start(bf16[256,896]{1,0:T(8,128)(2,1)S(1)} %shard_map.184), channel_id=1, source_target_pairs={{0,1},{1,2},{2,3},{3,4},{4,5},{5,6},{6,7},{8,9},{9,10},{10,11},{11... | collective-permute-start | bytes 1376264 | tf_op jit(solution)/shard_map/ppermute | solution.py:26
  98.2 0.0 collective-permute-done.4
  98.3 1.8 %add_convert_fusion = (bf16[2,224,896]{2,1,0:T(8,128)(2,1)S(1)}, bf16[2,224,896]{2,1,0:T(8,128)(2,1)S(1)}) fusion(bf16[2,448,896]{2,1,0:T(8,128)(2,1)} %collective-permute-done.4, bf16[2,448,896]{2,1,0:T(8,128)(2,1)S(1)} %copy-done.6), kind=kLoop, calls=%fused_computation.13 | loop fusion | flops 3211264 | bytes 4816896 | tf_op jit(solution)/shard_map/convert_element_type | solution.py:489
  100.0 0.0 copy-start.2
  100.1 0.0 copy-start.3
  100.1 0.0 collective-permute-done.3
  100.1 0.0 slice-start
  100.1 0.4 add_convert_fusion.1
  100.5 0.0 slice-start.1
  100.5 1.6 collective-permute-start.7
  102.1 1.5 collective-permute-start.6
  103.6 5.5 %collective-permute-done.5.refs_4_ = bf16[256,896]{1,0:T(8,128)(2,1)S(1)} collective-permute-done((bf16[256,896]{1,0:T(8,128)(2,1)S(1)}, bf16[256,896]{1,0:T(8,128)(2,1)S(1)}, u32[]{:S(2)}, u32[]{:S(2)}) %collective-permute-start.5) | collective-permute-done | bytes 458784 | tf_op jit(solution)/shard_map/ppermute | solution.py:26
  109.1 11.9 %shard_map.185 = bf16[320,1024]{1,0:T(8,128)(2,1)S(1)} custom-call(s32[5,2]{1,0:T(8,128)S(1)} %pad_add_fusion.place_ref, bf16[320,1024]{1,0:T(8,128)(2,1)S(1)} %fusion.9.q_ref, bf16[896,1024]{1,0:T(8,128)(2,1)S(1)} %copy-done.2, bf16[896,1024]{1,0:T(8,128)(2,1)S(1)} %copy-done.3, bf16[256,896]{1,0:T(8,128)(2,1)S(1)} %copy-done.1, ...), custom_call_target="tpu_custom_call" | custom-call | flops 10066329600 | bytes 5963776 | tf_op jit(solution)/shard_map/pallas_call | solution.py:197
  121.0 0.2 slice_select_fusion.context_ref
  121.2 4.5 %collective-permute-done.7 = bf16[2,224,896]{2,1,0:T(8,128)(2,1)S(1)} collective-permute-done((bf16[2,224,896]{2,1,0:T(8,128)(2,1)S(1)}, bf16[2,224,896]{2,1,0:T(8,128)(2,1)S(1)}, u32[]{:S(2)}, u32[]{:S(2)}) %collective-permute-start.7) | collective-permute-done | bytes 802848 | tf_op jit(solution)/shard_map/ppermute | solution.py:233
  125.7 0.2 add_convert_fusion.6
  125.9 0.0 collective-permute-done.6
  125.9 0.2 add_convert_fusion.7
  126.1 1.1 shard_map.187
  127.3 0.1 collective-permute-start.8
  127.3 2.5 %collective-permute-start.11 = (bf16[2,112,896]{2,1,0:T(8,128)(2,1)S(1)}, bf16[2,112,896]{2,1,0:T(8,128)(2,1)S(1)}, u32[]{:S(2)}, u32[]{:S(2)}) collective-permute-start(bf16[2,112,896]{2,1,0:T(8,128)(2,1)S(1)} %get-tuple-element.81), channel_id=1, source_target_pairs={{0,1},{1,0},{2,3},{3,2},{4,5},{5,4},{6,7},{7,6},{8,9},{9,8},{10,11... | collective-permute-start | bytes 1204232 | tf_op jit(solution)/shard_map/ppermute | solution.py:233
  129.9 0.5 collective-permute-start.12
  130.4 3.4 %copy-done = bf16[1024,4096]{1,0:T(8,128)(2,1)S(1)} copy-done((bf16[1024,4096]{1,0:T(8,128)(2,1)S(1)}, bf16[1024,4096]{1,0:T(8,128)(2,1)}, u32[]{:S(2)}) %copy-start) | copy-done | bytes 8388632
  133.8 1.1 shard_map.186
  134.9 1.0 add_convert_fusion.5
  135.9 1.1 shard_map.189
  137.0 0.1 collective-permute-start.9
  137.1 1.6 collective-permute-start.10
  138.7 1.1 shard_map.188
  139.8 0.0 collective-permute-done.11.a_came
  139.8 2.2 %collective-permute-done.12.b_came = bf16[2,112,896]{2,1,0:T(8,128)(2,1)S(1)} collective-permute-done((bf16[2,112,896]{2,1,0:T(8,128)(2,1)S(1)}, bf16[2,112,896]{2,1,0:T(8,128)(2,1)S(1)}, u32[]{:S(2)}, u32[]{:S(2)}) %collective-permute-start.12) | collective-permute-done | bytes 401440 | tf_op jit(solution)/shard_map/ppermute | solution.py:233
  142.0 0.2 shard_map.190
  142.3 1.2 collective-permute-start.13
  143.5 2.6 %collective-permute-start.14 = (bf16[4,28,896]{2,1,0:T(8,128)(2,1)S(1)}, bf16[4,28,896]{2,1,0:T(8,128)(2,1)S(1)}, u32[]{:S(2)}, u32[]{:S(2)}) collective-permute-start(bf16[4,28,896]{2,1,0:T(8,128)(2,1)S(1)} %get-tuple-element.86), channel_id=1, source_target_pairs={{0,4},{1,5},{2,6},{3,7},{4,0},{5,1},{6,2},{7,3},{8,12},{9,13},{10,... | collective-permute-start | bytes 602120 | tf_op jit(solution)/shard_map/ppermute | solution.py:555
  146.0 1.4 collective-permute-start.15
  147.4 5.4 %collective-permute-done.13.refs_1_ = bf16[4,28,896]{2,1,0:T(8,128)(2,1)S(1)} collective-permute-done((bf16[4,28,896]{2,1,0:T(8,128)(2,1)S(1)}, bf16[4,28,896]{2,1,0:T(8,128)(2,1)S(1)}, u32[]{:S(2)}, u32[]{:S(2)}) %collective-permute-start.13) | collective-permute-done | bytes 200736 | tf_op jit(solution)/shard_map/ppermute | solution.py:555
  152.7 7.5 %collective-permute-done.14.refs_2_ = bf16[4,28,896]{2,1,0:T(8,128)(2,1)S(1)} collective-permute-done((bf16[4,28,896]{2,1,0:T(8,128)(2,1)S(1)}, bf16[4,28,896]{2,1,0:T(8,128)(2,1)S(1)}, u32[]{:S(2)}, u32[]{:S(2)}) %collective-permute-start.14) | collective-permute-done | bytes 200736 | tf_op jit(solution)/shard_map/ppermute | solution.py:555
  160.2 0.0 collective-permute-done.15.refs_3_
  160.2 0.8 shard_map.191
  161.0 0.0 collective-permute-done.9
  161.0 0.0 collective-permute-done.10
  161.0 2.5 %add_convert_fusion.4 = bf16[256,1024]{1,0:T(8,128)(2,1)} fusion(bf16[256,1024]{1,0:T(8,128)(2,1)} %collective-permute-done.10, bf16[256,1024]{1,0:T(8,128)(2,1)} %collective-permute-done.9, bf16[256,1024]{1,0:T(8,128)(2,1)S(1)} %shard_map.188, bf16[256,4096]{1,0:T(8,128)(2,1)} %param.14, s32[]{:T(128)S(6)} %select_n.188), kind=kLoop, calls=%fused_computation.20 | loop fusion | flops 2097152 | bytes 2621444 | tf_op jit(solution)/shard_map/convert_element_type | solution.py:561
  (25 shorter events, 0.1 us)
Async XLA Ops:
  62.7 22.8 %collective-permute-start = (bf16[256,896]{1,0:T(8,128)(2,1)}, bf16[256,896]{1,0:T(8,128)(2,1)S(1)}, u32[]{:S(2)}, u32[]{:S(2)}) collective-permute-start(bf16[256,896]{1,0:T(8,128)(2,1)} %get-tuple-element.59.refs_0_), channel_id=1, source_target_pairs={{0,8},{8,0},{16,24},{24,16},{1,9},{9,1},{17,25},{25,17},{2,10},{10... | collective-permute-start | bytes 1376264 | tf_op jit(solution)/shard_map/ppermute | solution.py:233
  62.7 22.8 %collective-permute-start.1 = (bf16[256,896]{1,0:T(8,128)(2,1)}, bf16[256,896]{1,0:T(8,128)(2,1)S(1)}, u32[]{:S(2)}, u32[]{:S(2)}) collective-permute-start(bf16[256,896]{1,0:T(8,128)(2,1)} %get-tuple-element.59.refs_0_), channel_id=1, source_target_pairs={{0,16},{8,24},{16,0},{24,8},{1,17},{9,25},{17,1},{25,9},{2,18},{10... | collective-permute-start | bytes 1376264 | tf_op jit(solution)/shard_map/ppermute | solution.py:233
  64.2 21.3 %collective-permute-start.2 = (bf16[256,896]{1,0:T(8,128)(2,1)}, bf16[256,896]{1,0:T(8,128)(2,1)S(1)}, u32[]{:S(2)}, u32[]{:S(2)}) collective-permute-start(bf16[256,896]{1,0:T(8,128)(2,1)} %get-tuple-element.59.refs_0_), channel_id=1, source_target_pairs={{0,24},{8,16},{16,8},{24,0},{1,25},{9,17},{17,9},{25,1},{2,26},{10... | collective-permute-start | bytes 1376264 | tf_op jit(solution)/shard_map/ppermute | solution.py:233
  67.6 17.7 %copy-start.8 = (s32[4,2]{0,1:T(2,128)S(1)}, s32[4,2]{0,1:T(2,128)}, u32[]{:S(2)}) copy-start(s32[4,2]{0,1:T(2,128)} %param.27) | copy-start | bytes 100
  67.6 17.9 %copy-start.1 = (bf16[256,896]{1,0:T(8,128)(2,1)S(1)}, bf16[256,896]{1,0:T(8,128)(2,1)}, u32[]{:S(2)}) copy-start(bf16[256,896]{1,0:T(8,128)(2,1)} %get-tuple-element.59.refs_0_) | copy-start | bytes 1376260
  84.7 13.5 %collective-permute-start.4 = (bf16[2,448,896]{2,1,0:T(8,128)(2,1)}, bf16[2,448,896]{2,1,0:T(8,128)(2,1)}, u32[]{:S(2)}, u32[]{:S(2)}) collective-permute-start(bf16[2,448,896]{2,1,0:T(8,128)(2,1)} %get-tuple-element.67), channel_id=1, source_target_pairs={{0,8},{8,0},{16,24},{24,16},{1,9},{9,1},{17,25},{25,17},{2,10},{10... | collective-permute-start | bytes 4816904 | tf_op jit(solution)/shard_map/ppermute | solution.py:233
  85.1 15.0 %collective-permute-start.3 = (bf16[2,448,896]{2,1,0:T(8,128)(2,1)}, bf16[2,448,896]{2,1,0:T(8,128)(2,1)S(1)}, u32[]{:S(2)}, u32[]{:S(2)}) collective-permute-start(bf16[2,448,896]{2,1,0:T(8,128)(2,1)} %get-tuple-element.65), channel_id=1, source_target_pairs={{0,8},{8,0},{16,24},{24,16},{1,9},{9,1},{17,25},{25,17},{2,10},{10... | collective-permute-start | bytes 4816904 | tf_op jit(solution)/shard_map/ppermute | solution.py:233
  85.4 1.6 copy-start.4
  85.5 2.0 %copy-start.7 = (f32[4096]{0:T(1024)S(1)}, f32[4096]{0:T(1024)}, u32[]{:S(2)}) copy-start(f32[4096]{0:T(1024)} %param.15) | copy-start | bytes 49156
  88.2 10.1 %copy-start.6 = (bf16[2,448,896]{2,1,0:T(8,128)(2,1)S(1)}, bf16[2,448,896]{2,1,0:T(8,128)(2,1)}, u32[]{:S(2)}) copy-start(bf16[2,448,896]{2,1,0:T(8,128)(2,1)} %get-tuple-element.66) | copy-start | bytes 4816900
  94.7 5.4 %copy-start.5 = (bf16[2,448,896]{2,1,0:T(8,128)(2,1)S(1)}, bf16[2,448,896]{2,1,0:T(8,128)(2,1)}, u32[]{:S(2)}) copy-start(bf16[2,448,896]{2,1,0:T(8,128)(2,1)} %get-tuple-element.64) | copy-start | bytes 4816900
  94.7 14.4 %collective-permute-start.5 = (bf16[256,896]{1,0:T(8,128)(2,1)S(1)}, bf16[256,896]{1,0:T(8,128)(2,1)S(1)}, u32[]{:S(2)}, u32[]{:S(2)}) collective-permute-start(bf16[256,896]{1,0:T(8,128)(2,1)S(1)} %shard_map.184), channel_id=1, source_target_pairs={{0,1},{1,2},{2,3},{3,4},{4,5},{5,6},{6,7},{8,9},{9,10},{10,11},{11... | collective-permute-start | bytes 1376264 | tf_op jit(solution)/shard_map/ppermute | solution.py:26
  100.0 9.0 %copy-start.2 = (bf16[896,1024]{1,0:T(8,128)(2,1)S(1)}, bf16[896,1024]{1,0:T(8,128)(2,1)}, u32[]{:S(2)}) copy-start(bf16[896,1024]{1,0:T(8,128)(2,1)} %wk_ref.1) | copy-start | bytes 5505028
  100.1 9.0 %copy-start.3 = (bf16[896,1024]{1,0:T(8,128)(2,1)S(1)}, bf16[896,1024]{1,0:T(8,128)(2,1)}, u32[]{:S(2)}) copy-start(bf16[896,1024]{1,0:T(8,128)(2,1)} %wv_ref.1) | copy-start | bytes 5505028
  100.1 26.0 %slice-start = ((s8[8388608]{0:T(1024)(128)(4,1)}), s8[4194304]{0:T(1024)(128)(4,1)S(1)}, s32[]{:S(2)}) async-start(s8[8388608]{0:T(1024)(128)(4,1)} %bitcast.9), calls=%async_computation | async-start | bytes 8388608
  100.5 25.6 %slice-start.1 = ((s8[8388608]{0:T(1024)(128)(4,1)}), s8[4194304]{0:T(1024)(128)(4,1)S(1)}, s32[]{:S(2)}) async-start(s8[8388608]{0:T(1024)(128)(4,1)} %bitcast.9), calls=%async_computation.1 | async-start | bytes 8388608
  100.5 25.2 %collective-permute-start.7 = (bf16[2,224,896]{2,1,0:T(8,128)(2,1)S(1)}, bf16[2,224,896]{2,1,0:T(8,128)(2,1)S(1)}, u32[]{:S(2)}, u32[]{:S(2)}) collective-permute-start(bf16[2,224,896]{2,1,0:T(8,128)(2,1)S(1)} %get-tuple-element.74), channel_id=1, source_target_pairs={{0,1},{1,0},{2,3},{3,2},{4,5},{5,4},{6,7},{7,6},{8,9},{9,8},{10,11... | collective-permute-start | bytes 2408456 | tf_op jit(solution)/shard_map/ppermute | solution.py:233
  102.1 23.8 %collective-permute-start.6 = (bf16[2,224,896]{2,1,0:T(8,128)(2,1)S(1)}, bf16[2,224,896]{2,1,0:T(8,128)(2,1)S(1)}, u32[]{:S(2)}, u32[]{:S(2)}) collective-permute-start(bf16[2,224,896]{2,1,0:T(8,128)(2,1)S(1)} %get-tuple-element.72), channel_id=1, source_target_pairs={{0,16},{8,24},{16,0},{24,8},{1,17},{9,25},{17,1},{25,9},{2,18},{10... | collective-permute-start | bytes 2408456 | tf_op jit(solution)/shard_map/ppermute | solution.py:233
  127.3 7.7 %collective-permute-start.8 = (bf16[256,1024]{1,0:T(8,128)(2,1)S(1)}, bf16[256,1024]{1,0:T(8,128)(2,1)S(1)}, u32[]{:S(2)}, u32[]{:S(2)}) collective-permute-start(bf16[256,1024]{1,0:T(8,128)(2,1)S(1)} %shard_map.187), channel_id=1, source_target_pairs={{0,8},{8,0},{16,24},{24,16},{1,9},{9,1},{17,25},{25,17},{2,10},{10... | collective-permute-start | bytes 1572872 | tf_op jit(solution)/shard_map/ppermute | solution.py:233
  127.3 12.4 %collective-permute-start.11 = (bf16[2,112,896]{2,1,0:T(8,128)(2,1)S(1)}, bf16[2,112,896]{2,1,0:T(8,128)(2,1)S(1)}, u32[]{:S(2)}, u32[]{:S(2)}) collective-permute-start(bf16[2,112,896]{2,1,0:T(8,128)(2,1)S(1)} %get-tuple-element.81), channel_id=1, source_target_pairs={{0,1},{1,0},{2,3},{3,2},{4,5},{5,4},{6,7},{7,6},{8,9},{9,8},{10,11... | collective-permute-start | bytes 1204232 | tf_op jit(solution)/shard_map/ppermute | solution.py:233
  129.9 12.1 %collective-permute-start.12 = (bf16[2,112,896]{2,1,0:T(8,128)(2,1)S(1)}, bf16[2,112,896]{2,1,0:T(8,128)(2,1)S(1)}, u32[]{:S(2)}, u32[]{:S(2)}) collective-permute-start(bf16[2,112,896]{2,1,0:T(8,128)(2,1)S(1)} %get-tuple-element.83), channel_id=1, source_target_pairs={{0,16},{8,24},{16,0},{24,8},{1,17},{9,25},{17,1},{25,9},{2,18},{10... | collective-permute-start | bytes 1204232 | tf_op jit(solution)/shard_map/ppermute | solution.py:233
  130.4 3.4 %copy-start = (bf16[1024,4096]{1,0:T(8,128)(2,1)S(1)}, bf16[1024,4096]{1,0:T(8,128)(2,1)}, u32[]{:S(2)}) copy-start(bf16[1024,4096]{1,0:T(8,128)(2,1)} %weight_ref.7) | copy-start | bytes 25165828
  137.0 24.0 %collective-permute-start.9 = (bf16[256,1024]{1,0:T(8,128)(2,1)S(1)}, bf16[256,1024]{1,0:T(8,128)(2,1)}, u32[]{:S(2)}, u32[]{:S(2)}) collective-permute-start(bf16[256,1024]{1,0:T(8,128)(2,1)S(1)} %shard_map.189), channel_id=1, source_target_pairs={{0,8},{8,0},{16,24},{24,16},{1,9},{9,1},{17,25},{25,17},{2,10},{10... | collective-permute-start | bytes 1572872 | tf_op jit(solution)/shard_map/ppermute | solution.py:233
  137.1 23.9 %collective-permute-start.10 = (bf16[256,1024]{1,0:T(8,128)(2,1)}, bf16[256,1024]{1,0:T(8,128)(2,1)}, u32[]{:S(2)}, u32[]{:S(2)}) collective-permute-start(bf16[256,1024]{1,0:T(8,128)(2,1)} %add_convert_fusion.5), channel_id=1, source_target_pairs={{0,16},{8,24},{16,0},{24,8},{1,17},{9,25},{17,1},{25,9},{2,18},{10... | collective-permute-start | bytes 1572872 | tf_op jit(solution)/shard_map/ppermute | solution.py:233
  142.3 10.5 %collective-permute-start.13 = (bf16[4,28,896]{2,1,0:T(8,128)(2,1)S(1)}, bf16[4,28,896]{2,1,0:T(8,128)(2,1)S(1)}, u32[]{:S(2)}, u32[]{:S(2)}) collective-permute-start(bf16[4,28,896]{2,1,0:T(8,128)(2,1)S(1)} %get-tuple-element.85), channel_id=1, source_target_pairs={{0,2},{1,3},{2,4},{3,5},{4,6},{5,7},{6,0},{7,1},{8,10},{9,11},{10,... | collective-permute-start | bytes 602120 | tf_op jit(solution)/shard_map/ppermute | solution.py:555
  143.5 16.7 %collective-permute-start.14 = (bf16[4,28,896]{2,1,0:T(8,128)(2,1)S(1)}, bf16[4,28,896]{2,1,0:T(8,128)(2,1)S(1)}, u32[]{:S(2)}, u32[]{:S(2)}) collective-permute-start(bf16[4,28,896]{2,1,0:T(8,128)(2,1)S(1)} %get-tuple-element.86), channel_id=1, source_target_pairs={{0,4},{1,5},{2,6},{3,7},{4,0},{5,1},{6,2},{7,3},{8,12},{9,13},{10,... | collective-permute-start | bytes 602120 | tf_op jit(solution)/shard_map/ppermute | solution.py:555
  146.0 14.2 %collective-permute-start.15 = (bf16[4,28,896]{2,1,0:T(8,128)(2,1)S(1)}, bf16[4,28,896]{2,1,0:T(8,128)(2,1)S(1)}, u32[]{:S(2)}, u32[]{:S(2)}) collective-permute-start(bf16[4,28,896]{2,1,0:T(8,128)(2,1)S(1)} %get-tuple-element.87), channel_id=1, source_target_pairs={{0,6},{1,7},{2,0},{3,1},{4,2},{5,3},{6,4},{7,5},{8,14},{9,15},{10,... | collective-permute-start | bytes 602120 | tf_op jit(solution)/shard_map/ppermute | solution.py:555

commit v3 on v2

--- a/solution.py
+++ b/solution.py
@@ -298,12 +298,12 @@
 def gather_weights(blocks, count):
     height, width = blocks[0].shape
     out = jax.ShapeDtypeStruct((2, count * height, width), blocks[0].dtype)
-    anywhere = pl.BlockSpec(memory_space=pltpu.HBM)
+    resident = pl.BlockSpec(memory_space=pltpu.VMEM)
     return pl.pallas_call(
         gather_kernel,
         out_shape=[out, out],
-        in_specs=[anywhere] * 4,
-        out_specs=[anywhere] * 2,
+        in_specs=[resident] * 4,
+        out_specs=[resident] * 2,
         scratch_shapes=[
             pltpu.SemaphoreType.DMA((4,)),
             pltpu.SemaphoreType.DMA((5, 4)),

time: 166 us -> 147 us (0.89)
  Pallas kernels: 96 us -> 76.1 us
    pallas_call x1, Pallas kernels: 53.1 us -> 33.2 us  [gather_weights(): pl.pallas_call(gather_kernel, out_shape=[out, out], in_specs=[resident] *...]
  transfers between devices with their start and end apart: 16 -> 16, of which waited for: 5 -> 5; matrix products, arithmetic and copies ran while one was open for 9% -> 10% of each run, Pallas kernels for 21% -> 24%
where the time goes in v3:
time: 147 us; the launch traced here: 144 us
  Pallas kernels  76.1 us (52%)
  waiting for transfers between devices  25.4 us (17%)
  starting transfers between devices  18.9 us (13%)
  other arithmetic  10.5 us (7%)
  matrix products  6.47 us (4%)
  local copies, waits for them, and re-layouts  5.64 us (4%)
    pallas_call x1, Pallas kernels, gather_weights(): pl.pallas_call(gather_kernel, out_shape=[out, out], in_specs=[resident] *...  33.2 us
    pallas_call x2, Pallas kernels, one_call(): pl.pallas_call(kernel, out_shape=outs, in_specs=[vmem] * len(args), out_s...  24.8 us
    ppermute x3, waiting for transfers between devices, on_device(): parts.append(lax.ppermute(held[step], 'seq', moved))  13 us
    pallas_call x1, Pallas kernels, decode(): pl.pallas_call(decode_kernel, grid=(width // (HEADS_STEP * HD),), out_sha...  11.9 us
    ppermute x12, starting transfers between devices, swap(): return lax.ppermute(value, axis, [(i, i ^ distance) for i in range(count)])  10.4 us
    ppermute x12, waiting for transfers between devices, swap(): return lax.ppermute(value, axis, [(i, i ^ distance) for i in range(count)])  6.91 us
    dot_general x1, matrix products, matmul(): return jnp.dot(former, latter, preferred_element_type=jnp.float32)  6.47 us
    ppermute x1, waiting for transfers between devices, shifted(): lax.ppermute(value, axis, [(source, source + steps) for source in range(i...  5.46 us
  transfers between devices with their start and end apart: 16, of which 5 were waited for; matrix products, arithmetic and copies ran while one was open for 10% of the time, Pallas kernels for 24%

profile of v3, /device:TPU:0, one launch (start us, length us, event | category | flops | bytes accessed | tf_op | source)
XLA Modules:
  0.0 143.9 jit_solution(10598601631137755412)
XLA Ops:
  0.6 1.3 reshape.196.gain_ref
  1.9 33.2 %shard_map.181 = (bf16[2,896,896]{2,1,0:T(8,128)(2,1)}, bf16[2,896,896]{2,1,0:T(8,128)(2,1)}) custom-call(bf16[224,896]{1,0:T(8,128)(2,1)} %q_ref.1, bf16[224,896]{1,0:T(8,128)(2,1)} %k_ref.1, bf16[224,896]{1,0:T(8,128)(2,1)} %v_ref.1, bf16[224,896]{1,0:T(8,128)(2,1)} %o_ref.1), custom_call_target="tpu_custom_call" | custom-call | tf_op jit(solution)/shard_map/pallas_call | solution.py:302
  35.1 7.7 %shard_map.182 = (bf16[256,896]{1,0:T(8,128)(2,1)}, bf16[256,896]{1,0:T(8,128)(2,1)}, bf16[256,896]{1,0:T(8,128)(2,1)}, bf16[256,896]{1,0:T(8,128)(2,1)}, bf16[2...) custom-call(bf16[256,896]{1,0:T(8,128)(2,1)} %bitcast.11, f32[1,896]{1,0:T(1,128)} %reshape.196.gain_ref, ...), custom_call_target="tpu_custom_call" | custom-call | flops 2466250752 | bytes 11472384 | tf_op jit(solution)/shard_map/pallas_call | solution.py:220
  42.7 0.4 collective-permute-start
  43.1 1.3 collective-permute-start.1
  44.4 0.2 collective-permute-start.2
  44.6 1.5 %fusion.3.order_a_ref = bf16[896,896]{1,0:T(8,128)(2,1)} fusion(s32[896]{0:T(1024)S(1)} %get-tuple-element.101), kind=kLoop, calls=%fused_computation.7 | loop fusion | flops 1605632 | bytes 1609216 | tf_op jit(solution)/shard_map/convert_element_type | solution.py:462
  46.1 1.5 %fusion.4.order_b_ref = bf16[896,896]{1,0:T(8,128)(2,1)} fusion(s32[896]{0:T(1024)S(1)} %get-tuple-element.100), kind=kLoop, calls=%fused_computation.8 | loop fusion | flops 1605632 | bytes 1609216 | tf_op jit(solution)/shard_map/convert_element_type | solution.py:462
  47.7 17.1 %shard_map.183 = (bf16[256,896]{1,0:T(8,128)(2,1)}, bf16[2,448,896]{2,1,0:T(8,128)(2,1)}, bf16[2,448,896]{2,1,0:T(8,128)(2,1)}, bf16[2,448,896]{2,1,0:T(8,128)(2,1)}, bf16[2,448,896]{2,1,0:T(8,128)(2,1)}) custom-call(bf16[256,896]{1,0:T(8,128)(2,1)} %bitcast.12, f32[1,896]{1,0:T(1,128)} %reshape.196.gain_ref, bf16[256,896]{1,0:T(8,128)(2,1)} %bitcast.13, ...), custom_call_target="tpu_custom_call" | custom-call | flops 5754585088 | bytes 21564928 | tf_op jit(solution)/shard_map/pallas_call | solution.py:220
  64.8 0.7 collective-permute-start.4
  65.5 0.1 collective-permute-start.3
  65.5 0.1 copy.30
  65.6 0.1 pad.2.clone
  65.8 0.0 copy-start.7
  65.8 0.0 collective-permute-done.refs_1_
  65.8 0.0 collective-permute-done.1.refs_2_
  65.8 0.0 collective-permute-done.2.refs_3_
  65.8 0.7 shard_map.184
  66.5 0.8 copy-done.4
  67.3 0.5 fusion
  67.8 0.6 fusion.2
  68.5 6.5 %fusion.9.q_ref = bf16[320,1024]{1,0:T(8,128)(2,1)S(1)} fusion(bf16[4096,1024]{1,0:T(8,128)(2,1)} %param.16, bf16[256,4096]{1,0:T(8,128)(2,1)S(1)} %fusion.2, bf16[320]{0:T(512)(128)(2,1)S(1)} %pad.2.clone, bf16[320]{0:T(512)(128)(2,1)S(1)} %pad.clone), kind=kOutput, calls=%fused_computation.17 | convolution fusion | flops 2692546560 | bytes 11142400 | tf_op jit(solution)/shard_map/dot_general | solution.py:30
  75.0 3.4 %collective-permute-start.5 = (bf16[256,896]{1,0:T(8,128)(2,1)S(1)}, bf16[256,896]{1,0:T(8,128)(2,1)S(1)}, u32[]{:S(2)}, u32[]{:S(2)}) collective-permute-start(bf16[256,896]{1,0:T(8,128)(2,1)S(1)} %shard_map.184), channel_id=1, source_target_pairs={{0,1},{1,2},{2,3},{3,4},{4,5},{5,6},{6,7},{8,9},{9,10},{10,11},{11... | collective-permute-start | bytes 1376264 | tf_op jit(solution)/shard_map/ppermute | solution.py:26
  78.4 0.0 collective-permute-done.4
  78.4 1.8 %add_convert_fusion = (bf16[2,224,896]{2,1,0:T(8,128)(2,1)S(1)}, bf16[2,224,896]{2,1,0:T(8,128)(2,1)S(1)}) fusion(bf16[2,448,896]{2,1,0:T(8,128)(2,1)} %collective-permute-done.4, bf16[2,448,896]{2,1,0:T(8,128)(2,1)S(1)} %copy-done.6), kind=kLoop, calls=%fused_computation.13 | loop fusion | flops 3211264 | bytes 4816896 | tf_op jit(solution)/shard_map/convert_element_type | solution.py:489
  80.2 0.0 copy-start.2
  80.2 0.0 copy-start.3
  80.2 0.0 collective-permute-done.3
  80.2 0.0 slice-start
  80.2 0.4 add_convert_fusion.1
  80.6 0.0 slice-start.1
  80.6 1.7 %collective-permute-start.7 = (bf16[2,224,896]{2,1,0:T(8,128)(2,1)S(1)}, bf16[2,224,896]{2,1,0:T(8,128)(2,1)S(1)}, u32[]{:S(2)}, u32[]{:S(2)}) collective-permute-start(bf16[2,224,896]{2,1,0:T(8,128)(2,1)S(1)} %get-tuple-element.74), channel_id=1, source_target_pairs={{0,1},{1,0},{2,3},{3,2},{4,5},{5,4},{6,7},{7,6},{8,9},{9,8},{10,11... | collective-permute-start | bytes 2408456 | tf_op jit(solution)/shard_map/ppermute | solution.py:233
  82.4 1.3 collective-permute-start.6
  83.7 5.5 %collective-permute-done.5.refs_4_ = bf16[256,896]{1,0:T(8,128)(2,1)S(1)} collective-permute-done((bf16[256,896]{1,0:T(8,128)(2,1)S(1)}, bf16[256,896]{1,0:T(8,128)(2,1)S(1)}, u32[]{:S(2)}, u32[]{:S(2)}) %collective-permute-start.5) | collective-permute-done | bytes 458784 | tf_op jit(solution)/shard_map/ppermute | solution.py:26
  89.2 11.9 %shard_map.185 = bf16[320,1024]{1,0:T(8,128)(2,1)S(1)} custom-call(s32[5,2]{1,0:T(8,128)S(1)} %pad_add_fusion.place_ref, bf16[320,1024]{1,0:T(8,128)(2,1)S(1)} %fusion.9.q_ref, bf16[896,1024]{1,0:T(8,128)(2,1)S(1)} %copy-done.2, bf16[896,1024]{1,0:T(8,128)(2,1)S(1)} %copy-done.3, bf16[256,896]{1,0:T(8,128)(2,1)S(1)} %copy-done.1, ...), custom_call_target="tpu_custom_call" | custom-call | flops 10066329600 | bytes 5963776 | tf_op jit(solution)/shard_map/pallas_call | solution.py:197
  101.1 0.2 slice_select_fusion.context_ref
  101.3 4.6 %collective-permute-done.7 = bf16[2,224,896]{2,1,0:T(8,128)(2,1)S(1)} collective-permute-done((bf16[2,224,896]{2,1,0:T(8,128)(2,1)S(1)}, bf16[2,224,896]{2,1,0:T(8,128)(2,1)S(1)}, u32[]{:S(2)}, u32[]{:S(2)}) %collective-permute-start.7) | collective-permute-done | bytes 802848 | tf_op jit(solution)/shard_map/ppermute | solution.py:233
  105.9 0.2 add_convert_fusion.6
  106.1 0.0 collective-permute-done.6
  106.1 0.2 add_convert_fusion.7
  106.3 1.1 shard_map.187
  107.5 0.1 collective-permute-start.8
  107.6 2.5 %collective-permute-start.11 = (bf16[2,112,896]{2,1,0:T(8,128)(2,1)S(1)}, bf16[2,112,896]{2,1,0:T(8,128)(2,1)S(1)}, u32[]{:S(2)}, u32[]{:S(2)}) collective-permute-start(bf16[2,112,896]{2,1,0:T(8,128)(2,1)S(1)} %get-tuple-element.81), channel_id=1, source_target_pairs={{0,1},{1,0},{2,3},{3,2},{4,5},{5,4},{6,7},{7,6},{8,9},{9,8},{10,11... | collective-permute-start | bytes 1204232 | tf_op jit(solution)/shard_map/ppermute | solution.py:233
  110.1 0.5 collective-permute-start.12
  110.6 3.4 %copy-done = bf16[1024,4096]{1,0:T(8,128)(2,1)S(1)} copy-done((bf16[1024,4096]{1,0:T(8,128)(2,1)S(1)}, bf16[1024,4096]{1,0:T(8,128)(2,1)}, u32[]{:S(2)}) %copy-start) | copy-done | bytes 8388632
  114.0 1.1 shard_map.186
  115.1 0.0 collective-permute-done.8
  115.1 1.0 add_convert_fusion.5
  116.1 1.1 shard_map.189
  117.2 0.1 collective-permute-start.9
  117.3 1.6 %collective-permute-start.10 = (bf16[256,1024]{1,0:T(8,128)(2,1)}, bf16[256,1024]{1,0:T(8,128)(2,1)}, u32[]{:S(2)}, u32[]{:S(2)}) collective-permute-start(bf16[256,1024]{1,0:T(8,128)(2,1)} %add_convert_fusion.5), channel_id=1, source_target_pairs={{0,16},{8,24},{16,0},{24,8},{1,17},{9,25},{17,1},{25,9},{2,18},{10... | collective-permute-start | bytes 1572872 | tf_op jit(solution)/shard_map/ppermute | solution.py:233
  118.9 1.1 shard_map.188
  120.0 2.2 %collective-permute-done.12.b_came = bf16[2,112,896]{2,1,0:T(8,128)(2,1)S(1)} collective-permute-done((bf16[2,112,896]{2,1,0:T(8,128)(2,1)S(1)}, bf16[2,112,896]{2,1,0:T(8,128)(2,1)S(1)}, u32[]{:S(2)}, u32[]{:S(2)}) %collective-permute-start.12) | collective-permute-done | bytes 401440 | tf_op jit(solution)/shard_map/ppermute | solution.py:233
  122.2 0.2 shard_map.190
  122.5 1.2 collective-permute-start.13
  123.7 2.6 %collective-permute-start.14 = (bf16[4,28,896]{2,1,0:T(8,128)(2,1)S(1)}, bf16[4,28,896]{2,1,0:T(8,128)(2,1)S(1)}, u32[]{:S(2)}, u32[]{:S(2)}) collective-permute-start(bf16[4,28,896]{2,1,0:T(8,128)(2,1)S(1)} %get-tuple-element.86), channel_id=1, source_target_pairs={{0,4},{1,5},{2,6},{3,7},{4,0},{5,1},{6,2},{7,3},{8,12},{9,13},{10,... | collective-permute-start | bytes 602120 | tf_op jit(solution)/shard_map/ppermute | solution.py:555
  126.2 1.4 collective-permute-start.15
  127.6 5.4 %collective-permute-done.13.refs_1_ = bf16[4,28,896]{2,1,0:T(8,128)(2,1)S(1)} collective-permute-done((bf16[4,28,896]{2,1,0:T(8,128)(2,1)S(1)}, bf16[4,28,896]{2,1,0:T(8,128)(2,1)S(1)}, u32[]{:S(2)}, u32[]{:S(2)}) %collective-permute-start.13) | collective-permute-done | bytes 200736 | tf_op jit(solution)/shard_map/ppermute | solution.py:555
  133.0 7.6 %collective-permute-done.14.refs_2_ = bf16[4,28,896]{2,1,0:T(8,128)(2,1)S(1)} collective-permute-done((bf16[4,28,896]{2,1,0:T(8,128)(2,1)S(1)}, bf16[4,28,896]{2,1,0:T(8,128)(2,1)S(1)}, u32[]{:S(2)}, u32[]{:S(2)}) %collective-permute-start.14) | collective-permute-done | bytes 200736 | tf_op jit(solution)/shard_map/ppermute | solution.py:555
  140.6 0.0 collective-permute-done.15.refs_3_
  140.6 0.8 shard_map.191
  141.4 0.0 collective-permute-done.9
  141.4 0.0 collective-permute-done.10
  141.4 2.5 %add_convert_fusion.4 = bf16[256,1024]{1,0:T(8,128)(2,1)} fusion(bf16[256,1024]{1,0:T(8,128)(2,1)} %collective-permute-done.10, bf16[256,1024]{1,0:T(8,128)(2,1)} %collective-permute-done.9, bf16[256,1024]{1,0:T(8,128)(2,1)S(1)} %shard_map.188, bf16[256,4096]{1,0:T(8,128)(2,1)} %param.14, s32[]{:T(128)S(6)} %select_n.188), kind=kLoop, calls=%fused_computation.20 | loop fusion | flops 2097152 | bytes 2621444 | tf_op jit(solution)/shard_map/convert_element_type | solution.py:561
  (25 shorter events, 0.1 us)
Async XLA Ops:
  42.7 23.0 %collective-permute-start = (bf16[256,896]{1,0:T(8,128)(2,1)}, bf16[256,896]{1,0:T(8,128)(2,1)S(1)}, u32[]{:S(2)}, u32[]{:S(2)}) collective-permute-start(bf16[256,896]{1,0:T(8,128)(2,1)} %get-tuple-element.59.refs_0_), channel_id=1, source_target_pairs={{0,8},{8,0},{16,24},{24,16},{1,9},{9,1},{17,25},{25,17},{2,10},{10... | collective-permute-start | bytes 1376264 | tf_op jit(solution)/shard_map/ppermute | solution.py:233
  43.1 22.7 %collective-permute-start.1 = (bf16[256,896]{1,0:T(8,128)(2,1)}, bf16[256,896]{1,0:T(8,128)(2,1)S(1)}, u32[]{:S(2)}, u32[]{:S(2)}) collective-permute-start(bf16[256,896]{1,0:T(8,128)(2,1)} %get-tuple-element.59.refs_0_), channel_id=1, source_target_pairs={{0,16},{8,24},{16,0},{24,8},{1,17},{9,25},{17,1},{25,9},{2,18},{10... | collective-permute-start | bytes 1376264 | tf_op jit(solution)/shard_map/ppermute | solution.py:233
  44.4 21.4 %collective-permute-start.2 = (bf16[256,896]{1,0:T(8,128)(2,1)}, bf16[256,896]{1,0:T(8,128)(2,1)S(1)}, u32[]{:S(2)}, u32[]{:S(2)}) collective-permute-start(bf16[256,896]{1,0:T(8,128)(2,1)} %get-tuple-element.59.refs_0_), channel_id=1, source_target_pairs={{0,24},{8,16},{16,8},{24,0},{1,25},{9,17},{17,9},{25,1},{2,26},{10... | collective-permute-start | bytes 1376264 | tf_op jit(solution)/shard_map/ppermute | solution.py:233
  47.7 17.9 %copy-start.8 = (s32[4,2]{0,1:T(2,128)S(1)}, s32[4,2]{0,1:T(2,128)}, u32[]{:S(2)}) copy-start(s32[4,2]{0,1:T(2,128)} %param.27) | copy-start | bytes 100
  47.7 18.1 %copy-start.1 = (bf16[256,896]{1,0:T(8,128)(2,1)S(1)}, bf16[256,896]{1,0:T(8,128)(2,1)}, u32[]{:S(2)}) copy-start(bf16[256,896]{1,0:T(8,128)(2,1)} %get-tuple-element.59.refs_0_) | copy-start | bytes 1376260
  64.8 13.6 %collective-permute-start.4 = (bf16[2,448,896]{2,1,0:T(8,128)(2,1)}, bf16[2,448,896]{2,1,0:T(8,128)(2,1)}, u32[]{:S(2)}, u32[]{:S(2)}) collective-permute-start(bf16[2,448,896]{2,1,0:T(8,128)(2,1)} %get-tuple-element.67), channel_id=1, source_target_pairs={{0,8},{8,0},{16,24},{24,16},{1,9},{9,1},{17,25},{25,17},{2,10},{10... | collective-permute-start | bytes 4816904 | tf_op jit(solution)/shard_map/ppermute | solution.py:233
  65.5 14.7 %collective-permute-start.3 = (bf16[2,448,896]{2,1,0:T(8,128)(2,1)}, bf16[2,448,896]{2,1,0:T(8,128)(2,1)S(1)}, u32[]{:S(2)}, u32[]{:S(2)}) collective-permute-start(bf16[2,448,896]{2,1,0:T(8,128)(2,1)} %get-tuple-element.65), channel_id=1, source_target_pairs={{0,8},{8,0},{16,24},{24,16},{1,9},{9,1},{17,25},{25,17},{2,10},{10... | collective-permute-start | bytes 4816904 | tf_op jit(solution)/shard_map/ppermute | solution.py:233
  65.7 1.6 %copy-start.4 = (bf16[256,4096]{1,0:T(8,128)(2,1)S(1)}, bf16[256,4096]{1,0:T(8,128)(2,1)}, u32[]{:S(2)}) copy-start(bf16[256,4096]{1,0:T(8,128)(2,1)} %param.14) | copy-start | bytes 6291460
  65.8 2.0 %copy-start.7 = (f32[4096]{0:T(1024)S(1)}, f32[4096]{0:T(1024)}, u32[]{:S(2)}) copy-start(f32[4096]{0:T(1024)} %param.15) | copy-start | bytes 49156
  68.5 9.9 %copy-start.6 = (bf16[2,448,896]{2,1,0:T(8,128)(2,1)S(1)}, bf16[2,448,896]{2,1,0:T(8,128)(2,1)}, u32[]{:S(2)}) copy-start(bf16[2,448,896]{2,1,0:T(8,128)(2,1)} %get-tuple-element.66) | copy-start | bytes 4816900
  74.9 5.3 %copy-start.5 = (bf16[2,448,896]{2,1,0:T(8,128)(2,1)S(1)}, bf16[2,448,896]{2,1,0:T(8,128)(2,1)}, u32[]{:S(2)}) copy-start(bf16[2,448,896]{2,1,0:T(8,128)(2,1)} %get-tuple-element.64) | copy-start | bytes 4816900
  75.0 14.2 %collective-permute-start.5 = (bf16[256,896]{1,0:T(8,128)(2,1)S(1)}, bf16[256,896]{1,0:T(8,128)(2,1)S(1)}, u32[]{:S(2)}, u32[]{:S(2)}) collective-permute-start(bf16[256,896]{1,0:T(8,128)(2,1)S(1)} %shard_map.184), channel_id=1, source_target_pairs={{0,1},{1,2},{2,3},{3,4},{4,5},{5,6},{6,7},{8,9},{9,10},{10,11},{11... | collective-permute-start | bytes 1376264 | tf_op jit(solution)/shard_map/ppermute | solution.py:26
  80.2 9.0 %copy-start.2 = (bf16[896,1024]{1,0:T(8,128)(2,1)S(1)}, bf16[896,1024]{1,0:T(8,128)(2,1)}, u32[]{:S(2)}) copy-start(bf16[896,1024]{1,0:T(8,128)(2,1)} %wk_ref.1) | copy-start | bytes 5505028
  80.2 9.0 %copy-start.3 = (bf16[896,1024]{1,0:T(8,128)(2,1)S(1)}, bf16[896,1024]{1,0:T(8,128)(2,1)}, u32[]{:S(2)}) copy-start(bf16[896,1024]{1,0:T(8,128)(2,1)} %wv_ref.1) | copy-start | bytes 5505028
  80.2 26.1 %slice-start = ((s8[8388608]{0:T(1024)(128)(4,1)}), s8[4194304]{0:T(1024)(128)(4,1)S(1)}, s32[]{:S(2)}) async-start(s8[8388608]{0:T(1024)(128)(4,1)} %bitcast.9), calls=%async_computation | async-start | bytes 8388608
  80.6 25.7 %slice-start.1 = ((s8[8388608]{0:T(1024)(128)(4,1)}), s8[4194304]{0:T(1024)(128)(4,1)S(1)}, s32[]{:S(2)}) async-start(s8[8388608]{0:T(1024)(128)(4,1)} %bitcast.9), calls=%async_computation.1 | async-start | bytes 8388608
  80.6 25.3 %collective-permute-start.7 = (bf16[2,224,896]{2,1,0:T(8,128)(2,1)S(1)}, bf16[2,224,896]{2,1,0:T(8,128)(2,1)S(1)}, u32[]{:S(2)}, u32[]{:S(2)}) collective-permute-start(bf16[2,224,896]{2,1,0:T(8,128)(2,1)S(1)} %get-tuple-element.74), channel_id=1, source_target_pairs={{0,1},{1,0},{2,3},{3,2},{4,5},{5,4},{6,7},{7,6},{8,9},{9,8},{10,11... | collective-permute-start | bytes 2408456 | tf_op jit(solution)/shard_map/ppermute | solution.py:233
  82.4 23.7 %collective-permute-start.6 = (bf16[2,224,896]{2,1,0:T(8,128)(2,1)S(1)}, bf16[2,224,896]{2,1,0:T(8,128)(2,1)S(1)}, u32[]{:S(2)}, u32[]{:S(2)}) collective-permute-start(bf16[2,224,896]{2,1,0:T(8,128)(2,1)S(1)} %get-tuple-element.72), channel_id=1, source_target_pairs={{0,16},{8,24},{16,0},{24,8},{1,17},{9,25},{17,1},{25,9},{2,18},{10... | collective-permute-start | bytes 2408456 | tf_op jit(solution)/shard_map/ppermute | solution.py:233
  107.5 7.6 %collective-permute-start.8 = (bf16[256,1024]{1,0:T(8,128)(2,1)S(1)}, bf16[256,1024]{1,0:T(8,128)(2,1)S(1)}, u32[]{:S(2)}, u32[]{:S(2)}) collective-permute-start(bf16[256,1024]{1,0:T(8,128)(2,1)S(1)} %shard_map.187), channel_id=1, source_target_pairs={{0,8},{8,0},{16,24},{24,16},{1,9},{9,1},{17,25},{25,17},{2,10},{10... | collective-permute-start | bytes 1572872 | tf_op jit(solution)/shard_map/ppermute | solution.py:233
  107.6 12.4 %collective-permute-start.11 = (bf16[2,112,896]{2,1,0:T(8,128)(2,1)S(1)}, bf16[2,112,896]{2,1,0:T(8,128)(2,1)S(1)}, u32[]{:S(2)}, u32[]{:S(2)}) collective-permute-start(bf16[2,112,896]{2,1,0:T(8,128)(2,1)S(1)} %get-tuple-element.81), channel_id=1, source_target_pairs={{0,1},{1,0},{2,3},{3,2},{4,5},{5,4},{6,7},{7,6},{8,9},{9,8},{10,11... | collective-permute-start | bytes 1204232 | tf_op jit(solution)/shard_map/ppermute | solution.py:233
  110.1 12.1 %collective-permute-start.12 = (bf16[2,112,896]{2,1,0:T(8,128)(2,1)S(1)}, bf16[2,112,896]{2,1,0:T(8,128)(2,1)S(1)}, u32[]{:S(2)}, u32[]{:S(2)}) collective-permute-start(bf16[2,112,896]{2,1,0:T(8,128)(2,1)S(1)} %get-tuple-element.83), channel_id=1, source_target_pairs={{0,16},{8,24},{16,0},{24,8},{1,17},{9,25},{17,1},{25,9},{2,18},{10... | collective-permute-start | bytes 1204232 | tf_op jit(solution)/shard_map/ppermute | solution.py:233
  110.6 3.4 %copy-start = (bf16[1024,4096]{1,0:T(8,128)(2,1)S(1)}, bf16[1024,4096]{1,0:T(8,128)(2,1)}, u32[]{:S(2)}) copy-start(bf16[1024,4096]{1,0:T(8,128)(2,1)} %weight_ref.7) | copy-start | bytes 25165828
  117.2 24.2 %collective-permute-start.9 = (bf16[256,1024]{1,0:T(8,128)(2,1)S(1)}, bf16[256,1024]{1,0:T(8,128)(2,1)}, u32[]{:S(2)}, u32[]{:S(2)}) collective-permute-start(bf16[256,1024]{1,0:T(8,128)(2,1)S(1)} %shard_map.189), channel_id=1, source_target_pairs={{0,8},{8,0},{16,24},{24,16},{1,9},{9,1},{17,25},{25,17},{2,10},{10... | collective-permute-start | bytes 1572872 | tf_op jit(solution)/shard_map/ppermute | solution.py:233
  117.3 24.1 %collective-permute-start.10 = (bf16[256,1024]{1,0:T(8,128)(2,1)}, bf16[256,1024]{1,0:T(8,128)(2,1)}, u32[]{:S(2)}, u32[]{:S(2)}) collective-permute-start(bf16[256,1024]{1,0:T(8,128)(2,1)} %add_convert_fusion.5), channel_id=1, source_target_pairs={{0,16},{8,24},{16,0},{24,8},{1,17},{9,25},{17,1},{25,9},{2,18},{10... | collective-permute-start | bytes 1572872 | tf_op jit(solution)/shard_map/ppermute | solution.py:233
  122.5 10.5 %collective-permute-start.13 = (bf16[4,28,896]{2,1,0:T(8,128)(2,1)S(1)}, bf16[4,28,896]{2,1,0:T(8,128)(2,1)S(1)}, u32[]{:S(2)}, u32[]{:S(2)}) collective-permute-start(bf16[4,28,896]{2,1,0:T(8,128)(2,1)S(1)} %get-tuple-element.85), channel_id=1, source_target_pairs={{0,2},{1,3},{2,4},{3,5},{4,6},{5,7},{6,0},{7,1},{8,10},{9,11},{10,... | collective-permute-start | bytes 602120 | tf_op jit(solution)/shard_map/ppermute | solution.py:555
  123.7 16.9 %collective-permute-start.14 = (bf16[4,28,896]{2,1,0:T(8,128)(2,1)S(1)}, bf16[4,28,896]{2,1,0:T(8,128)(2,1)S(1)}, u32[]{:S(2)}, u32[]{:S(2)}) collective-permute-start(bf16[4,28,896]{2,1,0:T(8,128)(2,1)S(1)} %get-tuple-element.86), channel_id=1, source_target_pairs={{0,4},{1,5},{2,6},{3,7},{4,0},{5,1},{6,2},{7,3},{8,12},{9,13},{10,... | collective-permute-start | bytes 602120 | tf_op jit(solution)/shard_map/ppermute | solution.py:555
  126.2 14.4 %collective-permute-start.15 = (bf16[4,28,896]{2,1,0:T(8,128)(2,1)S(1)}, bf16[4,28,896]{2,1,0:T(8,128)(2,1)S(1)}, u32[]{:S(2)}, u32[]{:S(2)}) collective-permute-start(bf16[4,28,896]{2,1,0:T(8,128)(2,1)S(1)} %get-tuple-element.87), channel_id=1, source_target_pairs={{0,6},{1,7},{2,0},{3,1},{4,2},{5,3},{6,4},{7,5},{8,14},{9,15},{10,... | collective-permute-start | bytes 602120 | tf_op jit(solution)/shard_map/ppermute | solution.py:555
